TPU v7x, 32 devices: a whole 2x2x4 slice. The times are simulated.
32 devices in a mesh: expert: 8 (over z, y), wshard: 4 (over x, core).
Axes of the slice: x: 2, y: 2, z: 4, core: 2. Of those that a mesh axis runs over, the one named last changes fastest.
Arguments:
- tokens: bfloat16 [16384, 768], P(('expert', 'wshard')), may hold values from -6 to 6
- attn_norm: bfloat16 [768], P('wshard'), may hold values from 0.5 to 1.5
- attn_in: bfloat16 [768, 2304], P('wshard'), may hold values from -0.21875 to 0.21875
- attn_out: bfloat16 [768, 768], P('wshard'), may hold values from -6 to 6
- rel_bias: bfloat16 [32, 12], replicated, may hold values from -6 to 6
- buckets: int32 [4095], replicated, may hold values from 0 to 31
- ffn_norm: bfloat16 [768], P('wshard'), may hold values from 0.5 to 1.5
- router: bfloat16 [768, 8], P('wshard'), may hold values from -0.375 to 0.375
- routes: int32 [16384, 1], P(('expert', 'wshard')), may hold values from 0 to 7; in each aligned block of 512 rows (0 to 511, 512 to 1023, ...) at most 128 rows name the same one
- expert_in: bfloat16 [8, 768, 3072], P('expert'), may hold values from -0.21875 to 0.21875
- expert_out: bfloat16 [8, 3072, 768], P('expert'), may hold values from -2 to 2
- cotangent: bfloat16 [16384, 768], P(('expert', 'wshard')), may hold values from -6 to 6
Outputs:
- mixed: bfloat16 [16384, 768], P(('expert', 'wshard'))
- grad_tokens: float32 [16384, 768], P(('expert', 'wshard'))
- grad_attn_norm: float32 [768], P(('expert', 'wshard'))
- grad_attn_in: float32 [768, 2304], P(('expert', 'wshard'))
- grad_attn_out: float32 [768, 768], P(('expert', 'wshard'))
- grad_rel_bias: float32 [32, 12], replicated
- grad_ffn_norm: float32 [768], P(('expert', 'wshard'))
- grad_router: float32 [768, 8], P(('expert', 'wshard'))
- grad_expert_in: float32 [8, 768, 3072], P('expert', None, 'wshard')
- grad_expert_out: float32 [8, 3072, 768], P('expert', 'wshard')
Inputs may be any that keep to these rules, and one draw needn't show every extreme that they name: `routes`: among the rows of one device no expert is named by more than 128 rows, and on some device some expert is named by exactly 128.
All inputs are finite; a program needn't handle non-finite values.
Results may differ from a plain program's by a relative error of at most 0.015.
Values may be sent and summed in bfloat16 or wider, within the bound.
No kernel may reach another device: no remote copies, remote signals or barrier semaphores. Data moves between devices by JAX's collectives and lax.ppermute only.
A program may use at most 256 MiB of HBM per device.

v0:
```python
import functools
import math

import jax
import jax.numpy as jnp
from jax import lax
from jax.experimental import pallas as pl
from jax.experimental.pallas import tpu as pltpu
from jax.sharding import PartitionSpec as P

epsilon = 1e-06
highest = lax.Precision.HIGHEST
f32 = jnp.float32
bf16 = jnp.bfloat16
LOG2E = math.log2(math.e)
LANES = 128
BLOCK = 256


def rms_scale(values):
    return lax.rsqrt(jnp.mean(values * values, axis=-1, keepdims=True) + epsilon)


def norm_back(grad_normed, values, scale, gain):
    scaled = grad_normed * gain
    inner_mean = jnp.mean(scaled * values, axis=-1, keepdims=True)
    grad_values = scale * scaled - values * (scale * scale * scale) * inner_mean
    return (grad_values, jnp.sum(grad_normed * values * scale, axis=0))


def build_bias(offsets, bias_ref):
    chunks = offsets.shape[0]
    rows = jnp.broadcast_to(offsets[:, None, :], (chunks, 8, LANES)).reshape(chunks * 8, LANES)
    sub = lax.broadcasted_iota(jnp.int32, (chunks * 8, LANES), 0) % 8
    for bit in (1, 2, 4):
        rows = jnp.where((sub & bit) != 0, pltpu.roll(rows, bit, 1), rows)
    lane = lax.broadcasted_iota(jnp.int32, (8, LANES), 1)
    sub8 = lax.broadcasted_iota(jnp.int32, (8, LANES), 0)
    for part in range(LANES // 8):
        turned = pltpu.roll(rows, 8 * part, 1) if part else rows
        upper = lane >= sub8 + 8 * part
        for tile in range(chunks - 1):
            chunk = chunks - 1 - tile
            bias_ref[tile * LANES + 8 * part : tile * LANES + 8 * part + 8, :] = jnp.where(
                upper, turned[chunk * 8 : chunk * 8 + 8], turned[chunk * 8 - 8 : chunk * 8]
            )


def fold_bias(grad_ref, work_ref, chunks):
    lane = lax.broadcasted_iota(jnp.int32, (LANES, LANES), 1)
    sub = lax.broadcasted_iota(jnp.int32, (LANES, LANES), 0)
    upper = lane >= sub
    half = LANES // 2
    for chunk in range(chunks):
        total = None
        if chunk >= 1:
            start = (chunks - 1 - chunk) * LANES
            total = jnp.where(upper, grad_ref[start : start + LANES, :], 0.0)
        if chunk <= chunks - 2:
            start = (chunks - 2 - chunk) * LANES
            lower = jnp.where(upper, 0.0, grad_ref[start : start + LANES, :])
            total = lower if total is None else total + lower
        work_ref[0, chunk * half : (chunk + 1) * half, :] = total[:half]
        work_ref[1, chunk * half : (chunk + 1) * half, :] = total[half:]
    total = work_ref[0] + pltpu.roll(work_ref[1], LANES - half, 1)
    while half > 8:
        half //= 2
        total = total.reshape(chunks, 2, half, LANES)
        total = total[:, 0].reshape(chunks * half, LANES) + pltpu.roll(
            total[:, 1].reshape(chunks * half, LANES), LANES - half, 1
        )
    sub8 = lax.broadcasted_iota(jnp.int32, (chunks * 8, LANES), 0) % 8
    for bit in (1, 2, 4):
        total = jnp.where((sub8 & bit) != 0, pltpu.roll(total, LANES - bit, 1), total)
    return jnp.sum(total.reshape(chunks, 8, LANES), axis=1)


def split_scaled(query):
    scaled = query.astype(f32) * (0.125 * LOG2E)
    high = scaled.astype(bf16)
    low = (scaled - high.astype(f32)).astype(bf16)
    return jnp.concatenate([high, low], axis=0)


def strips(bias_ref, tiles, first, start, count):
    parts = []
    for index in range(count):
        row = (tiles - 1 - (first + index)) * LANES + start
        parts.append(bias_ref[pl.ds(pl.multiple_of(row, LANES), BLOCK), :])
    return jnp.concatenate(parts, axis=1)


def forward_kernel(
    offset_ref, query_ref, key_ref, value_ref, mixed_ref, log_ref, bias_ref, key2_ref, value_aug_ref,
    query2_ref, score_ref, weight_ref, top_ref, total_ref
):
    size, length = query_ref.shape
    tiles = length // LANES
    blocks = length // BLOCK
    across = BLOCK // LANES
    build_bias(offset_ref[0] * LOG2E, bias_ref)
    keys = key_ref[...].astype(f32).T.astype(bf16)
    key2_ref[...] = jnp.concatenate([keys, keys], axis=1)
    value_aug_ref[:size, :] = value_ref[...]
    extra = lax.broadcasted_iota(jnp.int32, (16, length), 0)
    value_aug_ref[size:, :] = jnp.where(extra == 0, 1.0, 0.0).astype(bf16)

    top_ref[...] = jnp.full(top_ref.shape, -jnp.inf, f32)
    total_ref[...] = jnp.zeros_like(total_ref)
    query2_ref[...] = split_scaled(query_ref[...])

    def score_chunk(chunk, carry):
        start = pl.multiple_of(chunk * BLOCK, BLOCK)
        rows = pl.ds(start, BLOCK)
        for block in range(blocks):
            columns = slice(block * BLOCK, (block + 1) * BLOCK)
            scores = jnp.dot(key2_ref[rows, :], query2_ref[:, columns], preferred_element_type=f32)
            scores = scores + strips(bias_ref, tiles, block * across, start, across)
            score_ref[rows, columns] = scores
            peak = jnp.max(scores.reshape(BLOCK // 8, 8, BLOCK), axis=0)
            top_ref[:, columns] = jnp.maximum(top_ref[:, columns], peak)
        return carry

    lax.fori_loop(0, blocks, score_chunk, 0)
    top = jnp.max(top_ref[...], axis=0, keepdims=True)
    top_ref[...] = jnp.broadcast_to(top, top_ref.shape)

    def value_chunk(chunk, carry):
        rows = pl.ds(pl.multiple_of(chunk * BLOCK, BLOCK), BLOCK)
        for block in range(blocks):
            columns = slice(block * BLOCK, (block + 1) * BLOCK)
            weight_ref[:, columns] = jnp.exp2(score_ref[rows, columns] - top_ref[:1, columns]).astype(bf16)
        total_ref[...] += jnp.dot(value_aug_ref[:, rows], weight_ref[...], preferred_element_type=f32)
        return carry

    lax.fori_loop(0, blocks, value_chunk, 0)
    row_total = total_ref[size : size + 1, :]
    mixed_ref[...] = (total_ref[:size, :] / row_total).astype(bf16)
    log_ref[0] = top + jnp.log2(row_total)


def backward_kernel(
    offset_ref,
    query_ref,
    key_ref,
    value_ref,
    grad_ref,
    mixed_ref,
    log_ref,
    dqkv_ref,
    doffset_ref,
    bias_ref,
    dbias_ref,
    query2_ref,
    query_rows_ref,
    grad_rows_ref,
    key2_ref,
    value_rows_ref,
    delta_ref,
    weight_ref,
    score_ref,
    dquery_acc_ref,
    fold_ref,
):
    size, length = query_ref.shape
    tiles = length // LANES
    blocks = length // BLOCK
    across = BLOCK // LANES
    build_bias(offset_ref[0] * LOG2E, bias_ref)
    dbias_ref[...] = jnp.zeros_like(dbias_ref)
    query2_ref[...] = split_scaled(query_ref[...])
    query_rows_ref[...] = query_ref[...].astype(f32).T.astype(bf16)
    grad = grad_ref[...].astype(f32)
    grad_rows_ref[...] = grad.T.astype(bf16)
    keys = key_ref[...].astype(f32).T.astype(bf16)
    key2_ref[...] = jnp.concatenate([keys, keys], axis=1)
    value_rows_ref[...] = value_ref[...].astype(f32).T.astype(bf16)
    delta_ref[...] = jnp.sum(grad * mixed_ref[...].astype(f32), axis=0, keepdims=True)
    dquery_acc_ref[...] = jnp.zeros_like(dquery_acc_ref)

    def one_chunk(chunk, carry):
        start = pl.multiple_of(chunk * BLOCK, BLOCK)
        rows = pl.ds(start, BLOCK)
        for block in range(blocks):
            columns = slice(block * BLOCK, (block + 1) * BLOCK)
            scores = jnp.dot(key2_ref[rows, :], query2_ref[:, columns], preferred_element_type=f32)
            scores = scores + strips(bias_ref, tiles, block * across, start, across)
            weights = jnp.exp2(scores - log_ref[0, :, columns])
            weight_ref[:, columns] = weights.astype(bf16)
            dweights = jnp.dot(value_rows_ref[rows, :], grad_ref[:, columns], preferred_element_type=f32)
            dscores = weights * (dweights - delta_ref[:, columns])
            for index in range(across):
                row = (tiles - 1 - (block * across + index)) * LANES + start
                place = pl.ds(pl.multiple_of(row, LANES), BLOCK)
                dbias_ref[place, :] += dscores[:, index * LANES : (index + 1) * LANES]
            score_ref[:, columns] = dscores.astype(bf16)
        dquery_acc_ref[...] += jnp.dot(key_ref[:, rows], score_ref[...], preferred_element_type=f32)
        dvalue = jnp.dot(weight_ref[...], grad_rows_ref[...], preferred_element_type=f32)
        dkey = jnp.dot(score_ref[...], query_rows_ref[...], preferred_element_type=f32) * 0.125
        dqkv_ref[2 * size :, rows] = dvalue.T.astype(bf16)
        dqkv_ref[size : 2 * size, rows] = dkey.T.astype(bf16)
        return carry

    lax.fori_loop(0, blocks, one_chunk, 0)
    dqkv_ref[:size, :] = (dquery_acc_ref[...] * 0.125).astype(bf16)
    doffset_ref[0] = fold_bias(dbias_ref, fold_ref, offset_ref.shape[1])


def attention_forward(offsets, qkv, heads):
    columns, length = qkv.shape
    size = columns // (3 * heads)
    chunks = offsets.shape[1]
    elements = heads * length * length
    return pl.pallas_call(
        forward_kernel,
        grid=(heads,),
        in_specs=[
            pl.BlockSpec((1, chunks, LANES), lambda h: (h, 0, 0)),
            pl.BlockSpec((size, length), lambda h: (h, 0)),
            pl.BlockSpec((size, length), lambda h: (heads + h, 0)),
            pl.BlockSpec((size, length), lambda h: (2 * heads + h, 0)),
        ],
        out_specs=[
            pl.BlockSpec((size, length), lambda h: (h, 0)),
            pl.BlockSpec((1, 1, length), lambda h: (h, 0, 0)),
        ],
        out_shape=[
            jax.ShapeDtypeStruct((heads * size, length), bf16),
            jax.ShapeDtypeStruct((heads, 1, length), f32),
        ],
        scratch_shapes=[
            pltpu.VMEM(((chunks - 1) * LANES, LANES), f32),
            pltpu.VMEM((length, 2 * size), bf16),
            pltpu.VMEM((size + 16, length), bf16),
            pltpu.VMEM((2 * size, length), bf16),
            pltpu.VMEM((length, length), f32),
            pltpu.VMEM((BLOCK, length), bf16),
            pltpu.VMEM((8, length), f32),
            pltpu.VMEM((size + 16, length), f32),
        ],
        compiler_params=pltpu.CompilerParams(vmem_limit_bytes=48 * 1024 * 1024),
        cost_estimate=pl.CostEstimate(
            flops=elements * 64 * 4 * 4, bytes_accessed=8 * 1024 * 1024, transcendentals=elements
        ),
    )(offsets, qkv, qkv, qkv)


def attention_backward(offsets, qkv, grad, mixed, logs, heads, first, count):
    columns, length = qkv.shape
    size = columns // (3 * heads)
    chunks = offsets.shape[1]
    elements = count * length * length
    rows = pl.BlockSpec((size, length), lambda h: (first + h, 0))
    return pl.pallas_call(
        backward_kernel,
        grid=(count,),
        in_specs=[
            pl.BlockSpec((1, chunks, LANES), lambda h: (first + h, 0, 0)),
            rows,
            pl.BlockSpec((size, length), lambda h: (heads + first + h, 0)),
            pl.BlockSpec((size, length), lambda h: (2 * heads + first + h, 0)),
            rows,
            rows,
            pl.BlockSpec((1, 1, length), lambda h: (first + h, 0, 0)),
        ],
        out_specs=[
            pl.BlockSpec((3 * size, length), lambda h: (h, 0)),
            pl.BlockSpec((1, chunks, LANES), lambda h: (h, 0, 0)),
        ],
        out_shape=[
            jax.ShapeDtypeStruct((count * 3 * size, length), bf16),
            jax.ShapeDtypeStruct((count, chunks, LANES), f32),
        ],
        scratch_shapes=[
            pltpu.VMEM(((chunks - 1) * LANES, LANES), f32),
            pltpu.VMEM(((chunks - 1) * LANES, LANES), f32),
            pltpu.VMEM((2 * size, length), bf16),
            pltpu.VMEM((length, size), bf16),
            pltpu.VMEM((length, size), bf16),
            pltpu.VMEM((length, 2 * size), bf16),
            pltpu.VMEM((length, size), bf16),
            pltpu.VMEM((1, length), f32),
            pltpu.VMEM((BLOCK, length), bf16),
            pltpu.VMEM((BLOCK, length), bf16),
            pltpu.VMEM((size, length), f32),
            pltpu.VMEM((2, chunks * LANES // 2, LANES), f32),
        ],
        compiler_params=pltpu.CompilerParams(vmem_limit_bytes=48 * 1024 * 1024),
        cost_estimate=pl.CostEstimate(
            flops=elements * 64 * 10 * 7, bytes_accessed=4 * 1024 * 1024, transcendentals=elements
        ),
    )(offsets, qkv, qkv, qkv, grad, mixed, logs)


def project_kernel(here_ref, gain_ref, *refs):
    shards = (len(refs) - 3) // 2
    tokens, weights = refs[:shards], refs[shards : 2 * shards]
    normed_ref, qkv_ref, weight_ref = refs[2 * shards :]
    here = here_ref[0]
    rows = qkv_ref.shape[1] // shards
    part = weights[0].shape[0]
    for index in range(shards):
        start = pl.multiple_of((here ^ index) * part, part)
        weight_ref[pl.ds(start, part), :] = weights[index][...]
    gain = gain_ref[...]
    for index in range(shards):
        start = pl.multiple_of((here ^ index) * rows, rows)
        values = tokens[index][:rows, :].astype(f32)
        normed = (values * rms_scale(values) * gain).astype(bf16)
        normed_ref[pl.ds(start, rows), :] = normed
        qkv_ref[:, pl.ds(start, rows)] = lax.dot_general(
            weight_ref[...], normed, (((0,), (1,)), ((), ())), preferred_element_type=f32
        ).astype(bf16)


def project(here, gain, tokens, weights, rows):
    shards = len(tokens)
    width, columns = gain.shape[0], weights[0].shape[1]
    whole = pl.BlockSpec(memory_space=pltpu.VMEM)
    return pl.pallas_call(
        project_kernel,
        in_specs=[pl.BlockSpec(memory_space=pltpu.SMEM)] + [whole] * (1 + 2 * shards),
        out_specs=[whole, whole],
        out_shape=[
            jax.ShapeDtypeStruct((shards * rows, width), bf16),
            jax.ShapeDtypeStruct((columns, shards * rows), bf16),
        ],
        scratch_shapes=[pltpu.VMEM((width, columns), bf16)],
        compiler_params=pltpu.CompilerParams(vmem_limit_bytes=48 * 1024 * 1024),
        cost_estimate=pl.CostEstimate(
            flops=2 * shards * rows * width * columns, bytes_accessed=12 * 1024 * 1024, transcendentals=0
        ),
    )(here.reshape(1), gain.reshape(1, width), *tokens, *weights)


def expert_kernel(
    index_ref,
    arrived_ref,
    router_ref,
    weight_ref,
    plain_ref,
    hidden_ref,
    sorted_ref,
    inner_ref,
    rows_ref,
    logits_ref,
    gate_out_ref,
    probs_ref,
    gate_ref,
    sum_ref,
    total_ref,
):
    step = pl.program_id(0)
    slots = arrived_ref.shape[0]
    experts = router_ref.shape[0]
    chunk = 256
    own = lax.broadcasted_iota(jnp.int32, (1, experts), 1) == index_ref[0]

    @pl.when(step == 0)
    def start():
        logits = lax.dot_general(
            arrived_ref[...], router_ref[...], (((1,), (1,)), ((), ())), preferred_element_type=f32
        )
        shifted = jnp.exp(logits - jnp.max(logits, axis=-1, keepdims=True))
        probs = shifted / jnp.sum(shifted, axis=-1, keepdims=True)
        probs_ref[...] = probs
        gate = jnp.sum(jnp.where(own, probs, 0.0), axis=-1, keepdims=True)
        gate_ref[...] = jnp.broadcast_to(gate, gate_ref.shape)
        sum_ref[...] = jnp.zeros_like(sum_ref)
        total_ref[...] = jnp.zeros_like(total_ref)

    for first in range(0, slots, chunk):
        rows = slice(first, first + chunk)
        inner = jnp.dot(arrived_ref[rows, :], weight_ref[...], preferred_element_type=f32)
        plain = plain_ref[rows, :]
        hidden, slope = gelu_parts(inner)
        low = hidden.astype(bf16)
        hidden_ref[rows, :] = low
        sorted_ref[rows, :] = low
        product = hidden * plain
        partial = product[:, :LANES]
        for lane in range(LANES, product.shape[1], LANES):
            partial = partial + product[:, lane : lane + LANES]
        sum_ref[rows, :] += partial
        grad = (slope * (gate_ref[rows, :1] * plain)).astype(bf16)
        inner_ref[rows, :] = grad
        total_ref[rows, :] += lax.dot_general(
            grad, weight_ref[...], (((1,), (1,)), ((), ())), preferred_element_type=f32
        )

    @pl.when(step == pl.num_programs(0) - 1)
    def finish():
        gate = gate_ref[:, :1]
        grad_gate = jnp.sum(sum_ref[...], axis=-1, keepdims=True)
        grad_logits = (probs_ref[...] * (jnp.where(own, grad_gate, 0.0) - gate * grad_gate)).astype(bf16)
        logits_ref[...] = grad_logits
        gate_out_ref[...] = gate
        rows_ref[...] = (
            total_ref[...] + jnp.dot(grad_logits, router_ref[...], preferred_element_type=f32)
        ).astype(bf16)


def expert_rows(owner, here, shards, arrived, router, weight, plain):
    slots, width = arrived.shape
    experts = router.shape[0]
    hidden_width = weight.shape[1]
    block = hidden_width // shards
    half = shards // 2

    def which(i, index):
        return index[1] ^ jnp.where(i < half, 2 * i + 1, 2 * (i - half))

    return pl.pallas_call(
        expert_kernel,
        grid_spec=pltpu.PrefetchScalarGridSpec(
            num_scalar_prefetch=1,
            grid=(shards,),
            in_specs=[
                pl.BlockSpec((slots, width), lambda i, index: (0, 0)),
                pl.BlockSpec((experts, width), lambda i, index: (0, 0)),
                pl.BlockSpec((width, block), lambda i, index: (0, which(i, index))),
                pl.BlockSpec((slots, block), lambda i, index: (0, which(i, index))),
            ],
            out_specs=[
                pl.BlockSpec((slots, block), lambda i, index: (0, which(i, index))),
                pl.BlockSpec((slots, block), lambda i, index: (0, i)),
                pl.BlockSpec((slots, block), lambda i, index: (0, i)),
                pl.BlockSpec((slots, width), lambda i, index: (0, 0)),
                pl.BlockSpec((slots, experts), lambda i, index: (0, 0)),
                pl.BlockSpec((slots, 1), lambda i, index: (0, 0)),
            ],
            scratch_shapes=[
                pltpu.VMEM((slots, experts), f32),
                pltpu.VMEM((slots, LANES), f32),
                pltpu.VMEM((slots, LANES), f32),
                pltpu.VMEM((slots, width), f32),
            ],
        ),
        out_shape=[
            jax.ShapeDtypeStruct((slots, hidden_width), bf16),
            jax.ShapeDtypeStruct((slots, hidden_width), bf16),
            jax.ShapeDtypeStruct((slots, hidden_width), bf16),
            jax.ShapeDtypeStruct((slots, width), bf16),
            jax.ShapeDtypeStruct((slots, experts), bf16),
            jax.ShapeDtypeStruct((slots, 1), f32),
        ],
        compiler_params=pltpu.CompilerParams(vmem_limit_bytes=52 * 1024 * 1024),
        cost_estimate=pl.CostEstimate(
            flops=4 * slots * width * hidden_width,
            bytes_accessed=32 * 1024 * 1024,
            transcendentals=slots * hidden_width,
        ),
    )(jnp.stack([owner, here]).astype(jnp.int32), arrived, router, weight, plain)


def weight_grad_kernel(small_ref, big_ref, sent_ref, kept_ref, turned_ref):
    step = pl.program_id(0)
    half = pl.num_programs(0) // 2

    @pl.when(step == 0)
    def start():
        turned_ref[...] = small_ref[...].astype(f32).T.astype(bf16)

    product = jnp.dot(turned_ref[...], big_ref[...], preferred_element_type=f32).astype(bf16)

    @pl.when(step < half)
    def store_sent():
        sent_ref[...] = product

    @pl.when(step >= half)
    def store_kept():
        kept_ref[...] = product


def weight_grad(small, big, shards):
    slots, width = small.shape
    block = big.shape[1] // shards
    half = shards // 2
    return pl.pallas_call(
        weight_grad_kernel,
        grid=(shards,),
        in_specs=[
            pl.BlockSpec((slots, width), lambda i: (0, 0)),
            pl.BlockSpec((slots, block), lambda i: (0, i)),
        ],
        out_specs=[
            pl.BlockSpec((width, block), lambda i: (0, jnp.minimum(i, half - 1))),
            pl.BlockSpec((width, block), lambda i: (0, jnp.maximum(i - half, 0))),
        ],
        out_shape=[jax.ShapeDtypeStruct((width, half * block), bf16)] * 2,
        scratch_shapes=[pltpu.VMEM((width, slots), bf16)],
        compiler_params=pltpu.CompilerParams(vmem_limit_bytes=48 * 1024 * 1024),
        cost_estimate=pl.CostEstimate(
            flops=slots * width, bytes_accessed=1024 * 1024, transcendentals=0
        ),
    )(small, big)


def gelu_parts(inner):
    root = math.sqrt(2.0 / math.pi)
    square = inner * inner
    share = 0.5 + 0.5 * jnp.tanh(inner * (root + (root * 0.044715) * square))
    hidden = inner * share
    slope = share + hidden * (1.0 - share) * (2.0 * root + (root * 6 * 0.044715) * square)
    return hidden, slope


def exchange(rows, axis):
    return lax.all_to_all(rows, axis, split_axis=0, concat_axis=0, tiled=True)


def swap(values, step, axis="wshard"):
    return lax.ppermute(values, axis, [(i, i ^ step) for i in range(lax.axis_size(axis))])


def ordered(pieces, here):
    bit = 1
    while bit < len(pieces):
        turned = (here & bit) != 0
        pieces = [jnp.where(turned, pieces[i ^ bit], pieces[i]) for i in range(len(pieces))]
        bit *= 2
    return pieces


def gather_rest(values, far, shards):
    found = {0: values, shards // 2: far}
    step = shards // 4
    while step >= 1:
        for index in list(found):
            found[index ^ step] = swap(found[index], step)
        step //= 2
    return [found[index] for index in range(shards)]


def exchange_pieces(piece_for, shards, here):
    return [piece_for(here)] + [swap(piece_for(here ^ step), step) for step in range(1, shards)]


def tie(*values):
    return lax.optimization_barrier(values)


def local(
    tokens,
    attn_norm,
    attn_in,
    attn_out,
    rel_bias,
    buckets,
    ffn_norm,
    router,
    routes,
    expert_in,
    expert_out,
    cotangent,
):
    shards = lax.axis_size("wshard")
    here = lax.axis_index("wshard")
    groups = lax.axis_size("expert")
    owner = lax.axis_index("expert")
    rows, width = tokens.shape
    length = rows * shards
    bucket_count, head_total = rel_bias.shape
    heads = head_total // shards
    part = width // shards
    size = part // heads
    experts = router.shape[1]
    capacity = max(2, 2 * rows // experts)

    small = jnp.concatenate([attn_norm, ffn_norm, router.T.reshape(-1)])
    small_rows = -(-small.shape[0] // (16 * width)) * 16
    small = jnp.pad(small, (0, small_rows * width - small.shape[0])).reshape(small_rows, width)
    with_small = jnp.concatenate([tokens, small], axis=0)
    far = swap(with_small, shards // 2)
    route_ids = routes[:, 0]
    route_hot = route_ids[:, None] == jnp.arange(experts, dtype=jnp.int32)[None, :]
    hot_counts = route_hot.astype(jnp.int32)
    slot_rank = jnp.sum((jnp.cumsum(hot_counts, axis=0) - 1) * hot_counts, axis=1)
    slot_index = route_ids * capacity + slot_rank
    slots = experts * capacity
    place = (jnp.arange(slots, dtype=jnp.int32)[:, None] == slot_index[None, :]).astype(bf16)

    def put_in_slots(values):
        placed = jnp.dot(place, values, preferred_element_type=f32).astype(bf16)
        return placed.reshape(experts, capacity, width)

    def dispatch(placed):
        return exchange(placed, "expert").reshape(slots, width)

    def collect(returned):
        return lax.dot_general(
            place, returned, (((0,), (0,)), ((), ())), preferred_element_type=f32
        )

    def send_back(values):
        return exchange(values.reshape(experts, capacity, width), "expert").reshape(slots, width)

    weight_in, weight_out = expert_in[0], expert_out[0]
    cot_slots = put_in_slots(cotangent)

    split_in = attn_in.reshape(part, 3, shards, heads, size)
    sorted_in = split_in.transpose(2, 0, 1, 3, 4).reshape(shards, part, 3 * part)
    sent_in = [
        lax.dynamic_index_in_dim(sorted_in, here ^ step, 0, keepdims=False) for step in range(shards)
    ]
    by_head = split_in.transpose(0, 3, 2, 1, 4).reshape(part, 3 * width)
    far, cot_slots, by_head, *unused = tie(far, cot_slots, by_head, *sent_in)
    gathered = gather_rest(with_small, far, shards)
    own_in = [sent_in[0]] + [swap(sent_in[step], step) for step in range(1, shards)]
    small_all = jnp.stack(ordered([piece[rows:] for piece in gathered], here)).reshape(shards, -1)
    gain_a = small_all[:, :part].reshape(width).astype(f32)
    gain_f = small_all[:, part : 2 * part].reshape(width).astype(f32)
    full_router = (
        small_all[:, 2 * part : (2 + experts) * part]
        .reshape(shards, experts, part)
        .transpose(1, 0, 2)
        .reshape(experts, width)
    )

    chunks = 2 * length // LANES
    offset_ids = jnp.concatenate([jnp.full((1,), -1, jnp.int32), buckets[::-1]])
    offset_table = (offset_ids[:, None] == jnp.arange(bucket_count, dtype=jnp.int32)[None, :]).astype(f32)
    own_bias = lax.dynamic_slice_in_dim(rel_bias, here * heads, heads, 1).astype(f32)
    offsets = jnp.einsum("bh,ob->ho", own_bias, offset_table, precision=highest).reshape(
        heads, chunks, LANES
    )
    seq_normed, qkv = project(here, gain_a, gathered, own_in, rows)
    qkv, by_head, attn_out, cot_slots = tie(qkv, by_head, attn_out, cot_slots)
    cot_rows = dispatch(cot_slots)
    far_out = swap(attn_out, shards // 2)
    far_in = swap(by_head, shards // 2)
    mixed_own, logs = attention_forward(offsets, qkv, heads)
    mixed_own, cot_rows, far_out, far_in = tie(mixed_own, cot_rows, far_out, far_in)
    out_pieces = gather_rest(attn_out, far_out, shards)
    in_pieces = gather_rest(by_head, far_in, shards)
    full_out = jnp.concatenate(ordered(out_pieces, here), axis=0)

    def token_columns(values):
        return lambda w: lax.dynamic_slice_in_dim(values, w * rows, rows, values.ndim - 1)

    mixed_heads = jnp.concatenate(
        ordered(exchange_pieces(token_columns(mixed_own), shards, here), here), axis=0
    )
    start_rows = tokens.astype(f32)
    branch = lax.dot_general(
        mixed_heads, full_out, (((0,), (0,)), ((), ())), preferred_element_type=f32
    )
    middle = start_rows + branch
    scale_f = rms_scale(middle)
    normed_f = (middle * scale_f * gain_f).astype(bf16)
    arrived = dispatch(put_in_slots(normed_f))

    def route_probs(values):
        logits = lax.dot_general(
            values, full_router, (((1,), (1,)), ((), ())), preferred_element_type=f32
        )
        shifted = jnp.exp(logits - jnp.max(logits, axis=-1, keepdims=True))
        return shifted / jnp.sum(shifted, axis=-1, keepdims=True)

    own_probs = route_probs(normed_f)
    gate_prob = jnp.sum(jnp.where(route_hot, own_probs, 0.0), axis=-1, keepdims=True)
    grad_plain = lax.dot_general(
        cot_rows, weight_out, (((1,), (1,)), ((), ())), preferred_element_type=f32
    )
    full_in = jnp.concatenate(ordered(in_pieces, here), axis=0)
    arrived, gate_prob, grad_plain, full_in = tie(arrived, gate_prob, grad_plain, full_in)

    hidden, hidden_sorted, grad_inner, row_grads, grad_logits, gate = expert_rows(
        owner, here, shards, arrived, full_router, weight_in, grad_plain
    )
    row_grads_back = send_back(row_grads)

    def scatter_first(sent, kept):
        sums = kept.astype(f32) + swap(sent, 1).astype(f32)
        pieces = jnp.split(sums, shards // 2, axis=1)
        step = 2
        while 2 * step < shards:
            pieces = [
                pieces[index] + swap(pieces[index + 1].astype(bf16), step).astype(f32)
                for index in range(0, len(pieces), 2)
            ]
            step *= 2
        return pieces[0], pieces[1].astype(bf16)

    grad_result = (gate * cot_rows.astype(f32)).astype(bf16)
    out_sent, out_kept = weight_grad(grad_result, hidden_sorted, shards)
    in_sent, in_kept = weight_grad(arrived, grad_inner, shards)
    results = jnp.dot(hidden, weight_out, preferred_element_type=f32).astype(bf16)
    local_router = lax.dot_general(
        arrived, grad_logits, (((0,), (0,)), ((), ())), preferred_element_type=f32
    )
    out_kept, out_other = scatter_first(out_sent, out_kept)
    in_kept, in_other = scatter_first(in_sent, in_kept)
    row_grads_back, out_other, in_kept, in_other, results, local_router = tie(
        row_grads_back, out_other, in_kept, in_other, results, local_router
    )
    results_back = send_back(results)

    grad_normed_f = collect(row_grads_back)
    grad_out = cotangent.astype(f32)
    grad_middle_norm, grad_gain_f = norm_back(grad_normed_f, middle, scale_f, gain_f)
    grad_middle = grad_out + grad_middle_norm
    grad_branch = grad_middle.astype(bf16)
    grad_mixed = lax.dot_general(
        full_out, grad_branch, (((1,), (1,)), ((), ())), preferred_element_type=f32
    ).astype(bf16)
    grad_slabs = grad_mixed.reshape(shards, part, rows)
    grad_own = jnp.concatenate(
        ordered(
            exchange_pieces(
                lambda w: lax.dynamic_index_in_dim(grad_slabs, w, 0, keepdims=False), shards, here
            ),
            here,
        ),
        axis=1,
    )
    slab = width // groups
    slim = slab // shards
    local_sums = jnp.dot(mixed_heads, grad_branch, preferred_element_type=f32).astype(bf16)
    local_sums = local_sums.reshape(groups, shards // 2, 2, slim, width)
    extras = jnp.concatenate([local_router, grad_gain_f[:, None]], axis=1).astype(bf16)
    extras = extras.reshape(groups, shards // 2, 2, slim, experts + 1)

    def rider(side):
        main = lax.dynamic_index_in_dim(local_sums, side, 2, keepdims=False).reshape(groups, -1, width)
        rest = lax.dynamic_index_in_dim(extras, side, 2, keepdims=False).reshape(groups, -1)
        rest_rows = -(-rest.shape[1] // (16 * width)) * 16
        rest = jnp.pad(rest, ((0, 0), (0, rest_rows * width - rest.shape[1])))
        return jnp.concatenate([main, rest.reshape(groups, rest_rows, width)], axis=1)

    side = here & 1
    rider_kept = rider(side)
    rider_got = swap(rider(1 - side), 1)
    grad_own, rider_kept, out_other, in_other = tie(grad_own, rider_kept, out_other, in_other)
    out_got = swap(out_other, shards // 2)
    in_got = swap(in_other, shards // 2)

    def run_heads(first, count, grad_own):
        grad_qkv, grad_offsets = attention_backward(
            offsets, qkv, grad_own, mixed_own, logs, heads, first, count
        )
        grad_offsets = jnp.einsum(
            "ob,ho->hb", offset_table, grad_offsets.reshape(count, -1), precision=highest
        )
        return grad_qkv, grad_offsets

    def attn_in_part(grad_qkv):
        return (
            lax.dot_general(seq_normed, grad_qkv, (((0,), (1,)), ((), ())), preferred_element_type=f32)
            .astype(bf16)
            .reshape(groups, slab, -1)
        )

    def token_share(pieces, first, count):
        grads = jnp.concatenate(
            [
                piece.reshape(count, 1, 3 * size, rows)
                for piece in ordered(list(pieces), here)
            ],
            axis=1,
        ).reshape(count * width, rows)
        return lax.dot_general(
            grads,
            full_in[:, first * width : (first + count) * width],
            (((0,), (1,)), ((), ())),
            preferred_element_type=f32,
        )

    early = heads - 1
    offset_grads = []
    grad_normed = None
    if early:
        grad_qkv, grad_offsets = run_heads(0, early, grad_own)
        offset_grads.append(grad_offsets)
        grad_own, grad_qkv, rider_got = tie(grad_own, grad_qkv, rider_got)
    riders = (rider_kept.astype(f32) + rider_got.astype(f32)).astype(bf16)
    if early:
        block = attn_in_part(grad_qkv)
        fold = block.shape[1] * block.shape[2] // width
        riders = jnp.concatenate([block.reshape(groups, fold, width), riders], axis=1)
        pieces = exchange_pieces(token_columns(grad_qkv), shards, here)
    riders_back = exchange(riders, "expert")
    grad_qkv, grad_offsets = run_heads(early, 1, grad_own)
    if early:
        grad_qkv, grad_offsets, results_back, out_got, in_got, *pieces = tie(
            grad_qkv, grad_offsets, results_back, out_got, in_got, *pieces
        )
    offset_grads.append(grad_offsets)
    last = attn_in_part(grad_qkv)
    extra = jnp.concatenate(offset_grads, axis=0).reshape(-1).astype(bf16)
    tail_rows = -(-extra.shape[0] // (16 * 3 * size)) * 16
    extra = jnp.pad(extra, (0, tail_rows * 3 * size - extra.shape[0]))
    extra = jnp.broadcast_to(extra.reshape(1, tail_rows, 3 * size), (groups, tail_rows, 3 * size))
    last = jnp.concatenate([last, extra], axis=1)
    grad_qkv, last, riders_back = tie(grad_qkv, last, riders_back)
    if early:
        results_back, last, *pieces = tie(results_back, last, *pieces)
        grad_normed = token_share(pieces, 0, early)
    pieces = exchange_pieces(token_columns(grad_qkv), shards, here)
    last_sum = jnp.sum(exchange(last, "expert").astype(f32), axis=0)
    share = token_share(pieces, early, 1)
    grad_normed = share if grad_normed is None else grad_normed + share

    expert_result = collect(results_back)
    mixed = (middle + gate_prob * expert_result).astype(bf16)

    some = jnp.sum(riders_back.astype(f32), axis=0)
    if early:
        attn_in_sum = some[:fold].reshape(slab, early * 3 * size)
        some = some[fold:]
    some_rows = (shards // 2) * slim
    some_out = some[:some_rows].reshape(shards // 2, slim, width)
    some_rest = some[some_rows:].reshape(-1)[: some_rows * (experts + 1)].reshape(
        shards // 2, slim, experts + 1
    )

    scale_a = rms_scale(start_rows)
    grad_start, unused = norm_back(grad_normed, start_rows, scale_a, gain_a)
    grad_tokens = grad_middle + grad_start

    own_offsets = last_sum[slab:].reshape(-1)[: heads * bucket_count]
    wide = last_sum[:slab]
    if early:
        wide = jnp.concatenate([attn_in_sum, wide], axis=1)
    tail_rows = -(-own_offsets.shape[0] // (8 * width)) * 8
    tail = jnp.pad(own_offsets, (0, tail_rows * width - own_offsets.shape[0])).reshape(
        tail_rows, width
    )
    wide = wide.reshape(shards, slim, 3 * part)

    def shares_of(w):
        def pick(values):
            return lax.dynamic_index_in_dim(values, w, 0, keepdims=False)

        return jnp.concatenate([pick(some_out), pick(some_rest)], axis=1)

    some = shares_of(here // 2)
    for step in range(1, shards // 2):
        some = some + swap(shares_of((here // 2) ^ step), 2 * step)
    sum_attn_out, sum_router, sum_gain_f = (
        some[:, :width],
        some[:, width : width + experts],
        some[:, width + experts],
    )
    final = ordered(
        exchange_pieces(
            lambda w: jnp.concatenate(
                [
                    jnp.pad(
                        lax.dynamic_index_in_dim(wide, w, 0, keepdims=False),
                        ((0, 0), (0, width - 3 * part)),
                    ),
                    tail,
                ],
                axis=0,
            ),
            shards,
            here,
        ),
        here,
    )
    sum_attn_in = (
        jnp.stack([piece[:slim, : 3 * part] for piece in final], axis=1)
        .reshape(slim, shards, heads, 3, size)
        .transpose(0, 3, 1, 2, 4)
        .reshape(slim, 3 * width)
    )
    grad_rel_bias = jnp.concatenate(
        [
            piece[slim:].reshape(-1)[: heads * bucket_count].reshape(heads, bucket_count)
            for piece in final
        ],
        axis=0,
    ).T
    first = (owner * shards + here) * slim
    own_rows = (
        lax.dynamic_slice_in_dim(full_in, first, slim, 0)
        .reshape(slim, heads, shards, 3, size)
        .transpose(0, 3, 2, 1, 4)
        .reshape(slim, 3 * width)
    )
    sum_gain_a = jnp.sum(own_rows.astype(f32) * sum_attn_in, axis=1) / lax.dynamic_slice_in_dim(
        gain_a, first, slim, 0
    )
    return (
        mixed,
        grad_tokens,
        sum_gain_a,
        sum_attn_in,
        sum_attn_out,
        grad_rel_bias,
        sum_gain_f,
        sum_router,
        (in_kept + in_got.astype(f32))[None],
        (out_kept + out_got.astype(f32)).T[None],
    )


def solution(mesh):
    placed = (
        P(("expert", "wshard"), None),
        P("wshard"),
        P("wshard", None),
        P("wshard", None),
        P(),
        P(),
        P("wshard"),
        P("wshard", None),
        P(("expert", "wshard"), None),
        P("expert", None, None),
        P("expert", None, None),
        P(("expert", "wshard"), None),
    )
    return jax.shard_map(
        local,
        mesh=mesh,
        in_specs=placed,
        out_specs=(
            P(("expert", "wshard"), None),
            P(("expert", "wshard"), None),
            P(("expert", "wshard")),
            P(("expert", "wshard"), None),
            P(("expert", "wshard"), None),
            P(),
            P(("expert", "wshard")),
            P(("expert", "wshard"), None),
            P("expert", None, "wshard"),
            P("expert", "wshard", None),
        ),
        check_vma=False,
    )
```

profile of v0, /device:TPU:0, one launch (start us, length us, event | category | flops | bytes accessed | tf_op | source)
XLA Modules:
  0.0 378.1 jit_solution(16468545420317416187)
XLA Ops:
  4.1 3.0 collective-permute-start
  7.1 2.3 copy.240
  9.4 2.4 copy.242
  11.9 2.1 constant_dynamic-slice_fusion.14
  20.0 2.4 copy.241
  22.6 2.2 fusion.11
  28.9 6.0 %collective-permute-done.4.refs_6_ = bf16[192,576]{1,0:T(8,128)(2,1)} collective-permute-done((bf16[192,576]{1,0:T(8,128)(2,1)}, bf16[192,576]{1,0:T(8,128)(2,1)}, u32[]{:S(2)}, u32[]{:S(2)}) %collective-permute-start.4) | collective-permute-done | bytes 221216 | tf_op jit(solution)/shard_map/ppermute | solution.py:513
  34.8 3.6 collective-permute-done.5.refs_7_
  38.4 5.6 %shard_map.195 = (bf16[2048,768]{1,0:T(8,128)(2,1)}, bf16[576,2048]{1,0:T(8,128)(2,1)}) custom-call(s32[1]{0:T(128)} %bitcast.here_ref, f32[1,768]{1,0:T(1,128)S(1)} %reshape.347.gain_ref, bf16[528,768]{1,0:T(8,128)(2,1)S(1)} %constant_dynamic-update-slice_fusion.refs_0_, bf16[528,768]{1,0:T(8,128)(2,1)S(1)} %collective-permute-done.2.refs_1_, ...), custom_call_target="tpu_custom_call" | custom-call | flops 1811939328 | bytes 12582912 | tf_op jit(solution)/shard_map/pallas_call | solution.py:320
  44.0 6.3 %all-to-all-start = ((bf16[8,128,768]{2,1,0:T(8,128)(2,1)}), bf16[8,128,768]{2,1,0:T(8,128)(2,1)}, u32[]{:S(2)}, u32[]{:S(2)}) async-start(bf16[8,128,768]{2,1,0:T(8,128)(2,1)} %bitcast.198), calls=%async_computation | async-start | bytes 3145728 | tf_op jit(solution)/shard_map/all_to_all | solution.py:509
  56.2 25.4 %shard_map.196 = (bf16[192,2048]{1,0:T(8,128)(2,1)S(1)}, f32[3,1,2048]{2,1,0:T(1,128)S(1)}) custom-call(f32[3,32,128]{2,1,0:T(8,128)S(1)} %bitcast.186, bf16[576,2048]{1,0:T(8,128)(2,1)S(1)} %copy-done.5, bf16[576,2048]{1,0:T(8,128)(2,1)S(1)} %copy-done.5, bf16[576,2048]{1,0:T(8,128)(2,1)S(1)} %copy-done.5), custom_call_target="tpu_custom_call" | custom-call | flops 12884901888 | bytes 8388608 | tf_op jit(solution)/shard_map/pallas_call | solution.py:214
  81.7 6.7 %all-to-all-done = bf16[8,128,768]{2,1,0:T(8,128)(2,1)} async-done(((bf16[8,128,768]{2,1,0:T(8,128)(2,1)}), bf16[8,128,768]{2,1,0:T(8,128)(2,1)}, u32[]{:S(2)}, u32[]{:S(2)}) %all-to-all-start) | async-done | bytes 1572896 | tf_op jit(solution)/shard_map/all_to_all | solution.py:509
  91.5 3.9 %collective-permute-done.8 = bf16[192,512]{1,0:T(8,128)(2,1)S(1)} collective-permute-done((bf16[192,512]{1,0:T(8,128)(2,1)S(1)}, bf16[192,512]{1,0:T(8,128)(2,1)S(1)}, u32[]{:S(2)}, u32[]{:S(2)}) %collective-permute-start.8) | collective-permute-done | bytes 196640 | tf_op jit(solution)/shard_map/ppermute | solution.py:513
  96.1 3.8 %collective-permute-done.9 = bf16[192,512]{1,0:T(8,128)(2,1)S(1)} collective-permute-done((bf16[192,512]{1,0:T(8,128)(2,1)S(1)}, bf16[192,512]{1,0:T(8,128)(2,1)S(1)}, u32[]{:S(2)}, u32[]{:S(2)}) %collective-permute-start.9) | collective-permute-done | bytes 196640 | tf_op jit(solution)/shard_map/ppermute | solution.py:513
  102.8 2.3 fusion.12
  105.1 4.2 %all-to-all-start.1 = ((bf16[8,128,768]{2,1,0:T(8,128)(2,1)}), bf16[8,128,768]{2,1,0:T(8,128)(2,1)S(1)}, u32[]{:S(2)}, u32[]{:S(2)}) async-start(bf16[8,128,768]{2,1,0:T(8,128)(2,1)} %bitcast.200), calls=%async_computation.1 | async-start | bytes 3145728 | tf_op jit(solution)/shard_map/all_to_all | solution.py:509
  109.3 10.2 %fusion.2.plain_ref = f32[1024,3072]{1,0:T(8,128)} fusion(bf16[1024,768]{1,0:T(8,128)(2,1)} %bitcast.16, bf16[1,3072,768]{2,1,0:T(8,128)(2,1)} %param.22), kind=kOutput, calls=%fused_computation.2 | convolution fusion | flops 4831838208 | bytes 18874368 | tf_op jit(solution)/shard_map/dot_general | solution.py:662
  120.6 2.3 broadcast_select_fusion.7
  122.9 2.0 pad_maximum_fusion
  124.8 21.3 %all-to-all-done.1 = bf16[8,128,768]{2,1,0:T(8,128)(2,1)S(1)} async-done(((bf16[8,128,768]{2,1,0:T(8,128)(2,1)}), bf16[8,128,768]{2,1,0:T(8,128)(2,1)S(1)}, u32[]{:S(2)}, u32[]{:S(2)}) %all-to-all-start.1) | async-done | bytes 1572896 | tf_op jit(solution)/shard_map/all_to_all | solution.py:509
  147.4 23.1 %shard_map.197 = (bf16[1024,3072]{1,0:T(8,128)(2,1)}, bf16[1024,3072]{1,0:T(8,128)(2,1)}, bf16[1024,3072]{1,0:T(8,128)(2,1)}, bf16[1024,768]{1,0:T(8,128)(2,1)},...) custom-call(s32[2]{0:T(128)S(1)} %pad_add_fusion.1.index_ref, bf16[1024,768]{1,0:T(8,128)(2,1)} %bitcast.182, ...), custom_call_target="tpu_custom_call" | custom-call | flops 9663676416 | bytes 33554432 | tf_op jit(solution)/shard_map/pallas_call | solution.py:413
  171.9 9.8 %shard_map.199 = (bf16[768,1536]{1,0:T(8,128)(2,1)}, bf16[768,1536]{1,0:T(8,128)(2,1)}) custom-call(bf16[1024,768]{1,0:T(8,128)(2,1)S(1)} %bitcast.183, bf16[1024,3072]{1,0:T(8,128)(2,1)} %get-tuple-element.95.big_ref), custom_call_target="tpu_custom_call" | custom-call | flops 786432 | bytes 1048576 | tf_op jit(solution)/shard_map/pallas_call | solution.py:479
  183.7 9.8 %shard_map.198 = (bf16[768,1536]{1,0:T(8,128)(2,1)}, bf16[768,1536]{1,0:T(8,128)(2,1)}) custom-call(bf16[1024,768]{1,0:T(8,128)(2,1)S(1)} %multiply_convert_fusion.small_ref, bf16[1024,3072]{1,0:T(8,128)(2,1)} %get-tuple-element.92.big_ref), custom_call_target="tpu_custom_call" | custom-call | flops 786432 | bytes 1048576 | tf_op jit(solution)/shard_map/pallas_call | solution.py:479
  194.0 4.6 %all-to-all-start.2 = ((bf16[8,128,768]{2,1,0:T(8,128)(2,1)}), bf16[8,128,768]{2,1,0:T(8,128)(2,1)}, u32[]{:S(2)}, u32[]{:S(2)}) async-start(bf16[8,128,768]{2,1,0:T(8,128)(2,1)} %bitcast.199), calls=%async_computation.2 | async-start | bytes 3145728 | tf_op jit(solution)/shard_map/all_to_all | solution.py:509
  201.0 9.5 %fusion.13 = bf16[1024,768]{1,0:T(8,128)(2,1)} fusion(bf16[1024,3072]{1,0:T(8,128)(2,1)} %get-tuple-element.98, bf16[1,3072,768]{2,1,0:T(8,128)(2,1)} %param.22), kind=kOutput, calls=%fused_computation.27 | convolution fusion | flops 4832624640 | bytes 12582912 | tf_op jit(solution)/shard_map/dot_general | solution.py:688
  210.5 2.3 convert_add_fusion
  212.9 2.2 copy-done.8
  217.2 2.3 convert_add_fusion.1
  219.5 2.2 copy-done.9
  222.9 13.1 %all-to-all-done.2 = bf16[8,128,768]{2,1,0:T(8,128)(2,1)} async-done(((bf16[8,128,768]{2,1,0:T(8,128)(2,1)}), bf16[8,128,768]{2,1,0:T(8,128)(2,1)}, u32[]{:S(2)}, u32[]{:S(2)}) %all-to-all-start.2) | async-done | bytes 1572896 | tf_op jit(solution)/shard_map/all_to_all | solution.py:509
  236.0 2.9 multiply_reduce_fusion
  249.2 4.5 %all-to-all-start.3 = ((bf16[8,128,768]{2,1,0:T(8,128)(2,1)}), bf16[8,128,768]{2,1,0:T(8,128)(2,1)}, u32[]{:S(2)}, u32[]{:S(2)}) async-start(bf16[8,128,768]{2,1,0:T(8,128)(2,1)} %bitcast.197), calls=%async_computation.3 | async-start | bytes 3145728 | tf_op jit(solution)/shard_map/all_to_all | solution.py:509
  253.8 3.5 collective-permute-done.18
  261.4 28.8 %shard_map.200 = (bf16[384,2048]{1,0:T(8,128)(2,1)S(1)}, f32[2,32,128]{2,1,0:T(8,128)S(1)}) custom-call(f32[3,32,128]{2,1,0:T(8,128)S(1)} %bitcast.187, bf16[576,2048]{1,0:T(8,128)(2,1)S(1)} %copy-done.6, bf16[576,2048]{1,0:T(8,128)(2,1)S(1)} %copy-done.6, bf16[576,2048]{1,0:T(8,128)(2,1)S(1)} %copy-done.6, ...), custom_call_target="tpu_custom_call" | custom-call | flops 37580963840 | bytes 4194304 | tf_op jit(solution)/shard_map/pallas_call | solution.py:254
  293.6 1.8 convolution_convert_fusion.2
  299.0 4.5 %all-to-all-start.4 = ((bf16[8,112,768]{2,1,0:T(8,128)(2,1)}), bf16[8,112,768]{2,1,0:T(8,128)(2,1)}, u32[]{:S(2)}, u32[]{:S(2)}) async-start(bf16[8,112,768]{2,1,0:T(8,128)(2,1)} %pad_maximum_fusion.2), calls=%async_computation.4 | async-start | bytes 2752512 | tf_op jit(solution)/shard_map/all_to_all | solution.py:509
  305.2 14.4 %shard_map.201 = (bf16[192,2048]{1,0:T(8,128)(2,1)S(1)}, f32[1,32,128]{2,1,0:T(8,128)S(1)}) custom-call(f32[3,32,128]{2,1,0:T(8,128)S(1)} %bitcast.188, bf16[576,2048]{1,0:T(8,128)(2,1)S(1)} %copy-done.7, bf16[576,2048]{1,0:T(8,128)(2,1)S(1)} %copy-done.7, bf16[576,2048]{1,0:T(8,128)(2,1)S(1)} %copy-done.7, ...), custom_call_target="tpu_custom_call" | custom-call | flops 18790481920 | bytes 4194304 | tf_op jit(solution)/shard_map/pallas_call | solution.py:254
  320.0 2.2 collective-permute-done.24
  322.2 6.4 %collective-permute-done.25 = bf16[384,512]{1,0:T(8,128)(2,1)} collective-permute-done((bf16[384,512]{1,0:T(8,128)(2,1)}, bf16[384,512]{1,0:T(8,128)(2,1)}, u32[]{:S(2)}, u32[]{:S(2)}) %collective-permute-start.25) | collective-permute-done | bytes 393248 | tf_op jit(solution)/shard_map/ppermute | solution.py:513
  328.6 4.2 %fusion.4 = (f32[1,768,768]{1,2,0:T(8,128)S(1)}, f32[1,768,768]{2,1,0:T(8,128)}) fusion(f32[768,1536]{1,0:T(8,128)} %copy-done.9, bf16[768,768]{1,0:T(8,128)(2,1)} %collective-permute-done.21, f32[768,768]{1,0:T(8,128)S(1)} %slice-done, bf16[768,768]{1,0:T(8,128)(2,1)} %collective-permute-done.22), kind=kLoop, calls=%fused_computation.14 | loop fusion | flops 2359296 | bytes 11796480 | tf_op jit(solution)/shard_map/broadcast_in_dim | solution.py:895
  332.8 1.9 copy.277
  334.7 2.7 convolution_convert_fusion.3
  340.9 4.2 %all-to-all-start.5 = ((bf16[8,112,192]{1,2,0:T(8,128)(2,1)}), bf16[8,112,192]{1,2,0:T(8,128)(2,1)S(1)}, u32[]{:S(2)}, u32[]{:S(2)}) async-start(bf16[8,112,192]{1,2,0:T(8,128)(2,1)} %pad_maximum_fusion.9), calls=%async_computation.5 | async-start | bytes 786432 | tf_op jit(solution)/shard_map/all_to_all | solution.py:509
  352.2 2.6 fusion.5
  354.8 3.6 add_convert_fusion
  362.4 3.3 fusion.16
  368.5 2.9 fusion.19
  371.4 2.1 collective-permute-done.30
  (333 shorter events, 82.2 us)
Async XLA Ops:
  0.6 50.0 %copy-start = (bf16[32,12]{0,1:T(8,128)(2,1)S(1)}, bf16[32,12]{0,1:T(8,128)(2,1)}, u32[]{:S(2)}) copy-start(bf16[32,12]{0,1:T(8,128)(2,1)} %param.16) | copy-start | bytes 2308
  4.1 21.1 %collective-permute-start = (bf16[528,768]{1,0:T(8,128)(2,1)S(1)}, bf16[528,768]{1,0:T(8,128)(2,1)S(1)}, u32[]{:S(2)}, u32[]{:S(2)}) collective-permute-start(bf16[528,768]{1,0:T(8,128)(2,1)S(1)} %constant_dynamic-update-slice_fusion.refs_0_), channel_id=1, source_target_pairs={{0,2},{1,3},{2,0},{3,1},{4,6},{5,7},{6,4},{7,5},{8,10},{9,11},{10,... | collective-permute-start | bytes 2433032 | tf_op jit(solution)/shard_map/ppermute | solution.py:513
  7.1 20.3 %collective-permute-start.2 = (bf16[528,768]{1,0:T(8,128)(2,1)S(1)}, bf16[528,768]{1,0:T(8,128)(2,1)S(1)}, u32[]{:S(2)}, u32[]{:S(2)}) collective-permute-start(bf16[528,768]{1,0:T(8,128)(2,1)S(1)} %constant_dynamic-update-slice_fusion.refs_0_), channel_id=1, source_target_pairs={{0,1},{1,0},{2,3},{3,2},{4,5},{5,4},{6,7},{7,6},{8,9},{9,8},{10,11... | collective-permute-start | bytes 2433032 | tf_op jit(solution)/shard_map/ppermute | solution.py:513
  25.2 2.7 collective-permute-start.1
  25.3 3.6 collective-permute-start.3
  25.7 9.1 %collective-permute-start.4 = (bf16[192,576]{1,0:T(8,128)(2,1)}, bf16[192,576]{1,0:T(8,128)(2,1)}, u32[]{:S(2)}, u32[]{:S(2)}) collective-permute-start(bf16[192,576]{1,0:T(8,128)(2,1)} %bitcast.14), channel_id=1, source_target_pairs={{0,2},{1,3},{2,0},{3,1},{4,6},{5,7},{6,4},{7,5},{8,10},{9,11},{10,... | collective-permute-start | bytes 663560 | tf_op jit(solution)/shard_map/ppermute | solution.py:513
  27.4 11.0 %collective-permute-start.5 = (bf16[192,576]{1,0:T(8,128)(2,1)}, bf16[192,576]{1,0:T(8,128)(2,1)}, u32[]{:S(2)}, u32[]{:S(2)}) collective-permute-start(bf16[192,576]{1,0:T(8,128)(2,1)} %bitcast.15), channel_id=1, source_target_pairs={{0,3},{1,2},{2,1},{3,0},{4,7},{5,6},{6,5},{7,4},{8,11},{9,10},{10,... | collective-permute-start | bytes 663560 | tf_op jit(solution)/shard_map/ppermute | solution.py:513
  44.0 44.3 %all-to-all-start = ((bf16[8,128,768]{2,1,0:T(8,128)(2,1)}), bf16[8,128,768]{2,1,0:T(8,128)(2,1)}, u32[]{:S(2)}, u32[]{:S(2)}) async-start(bf16[8,128,768]{2,1,0:T(8,128)(2,1)} %bitcast.198), calls=%async_computation | async-start | bytes 3145728 | tf_op jit(solution)/shard_map/all_to_all | solution.py:509
  50.9 30.7 %collective-permute-start.6 = (bf16[192,768]{1,0:T(8,128)(2,1)S(1)}, bf16[192,768]{1,0:T(8,128)(2,1)}, u32[]{:S(2)}, u32[]{:S(2)}) collective-permute-start(bf16[192,768]{1,0:T(8,128)(2,1)S(1)} %copy-done.35), channel_id=1, source_target_pairs={{0,2},{1,3},{2,0},{3,1},{4,6},{5,7},{6,4},{7,5},{8,10},{9,11},{10,... | collective-permute-start | bytes 884744 | tf_op jit(solution)/shard_map/ppermute | solution.py:513
  52.5 47.8 %collective-permute-start.12 = (bf16[192,768]{1,0:T(8,128)(2,1)S(1)}, bf16[192,768]{1,0:T(8,128)(2,1)}, u32[]{:S(2)}, u32[]{:S(2)}) collective-permute-start(bf16[192,768]{1,0:T(8,128)(2,1)S(1)} %copy-done.35), channel_id=1, source_target_pairs={{0,1},{1,0},{2,3},{3,2},{4,5},{5,4},{6,7},{7,6},{8,9},{9,8},{10,11... | collective-permute-start | bytes 884744 | tf_op jit(solution)/shard_map/ppermute | solution.py:513
  54.0 27.6 %collective-permute-start.7 = (bf16[192,2304]{1,0:T(8,128)(2,1)}, bf16[192,2304]{1,0:T(8,128)(2,1)}, u32[]{:S(2)}, u32[]{:S(2)}) collective-permute-start(bf16[192,2304]{1,0:T(8,128)(2,1)} %copy.247), channel_id=1, source_target_pairs={{0,2},{1,3},{2,0},{3,1},{4,6},{5,7},{6,4},{7,5},{8,10},{9,11},{10,... | collective-permute-start | bytes 2654216 | tf_op jit(solution)/shard_map/ppermute | solution.py:513
  56.2 34.4 %copy-start.30 = (bf16[1,1,16,768]{3,1,2,0:T(2,128)(2,1)S(1)}, bf16[1,1,16,768]{3,1,2,0:T(2,128)(2,1)}, u32[]{:S(2)}) copy-start(bf16[1,1,16,768]{3,1,2,0:T(2,128)(2,1)} %copy-done.29) | copy-start | bytes 73732
  56.2 34.4 %copy-start.32 = (bf16[1,1,16,768]{3,1,2,0:T(2,128)(2,1)S(1)}, bf16[1,1,16,768]{3,1,2,0:T(2,128)(2,1)}, u32[]{:S(2)}) copy-start(bf16[1,1,16,768]{3,1,2,0:T(2,128)(2,1)} %copy-done.31) | copy-start | bytes 73732
  56.2 34.4 %copy-start.34 = (bf16[1,1,16,768]{3,1,2,0:T(2,128)(2,1)S(1)}, bf16[1,1,16,768]{3,1,2,0:T(2,128)(2,1)}, u32[]{:S(2)}) copy-start(bf16[1,1,16,768]{3,1,2,0:T(2,128)(2,1)} %copy-done.33) | copy-start | bytes 73732
  56.2 34.7 %copy-start.52 = (f32[4,192]{1,0:T(4,128)S(1)}, f32[4,192]{1,0:T(4,128)}, u32[]{:S(2)}) copy-start(f32[4,192]{1,0:T(4,128)} %get-tuple-element.279) | copy-start | bytes 9220
  88.4 2.6 collective-permute-start.10
  88.5 6.8 %collective-permute-start.8 = (bf16[192,512]{1,0:T(8,128)(2,1)S(1)}, bf16[192,512]{1,0:T(8,128)(2,1)S(1)}, u32[]{:S(2)}, u32[]{:S(2)}) collective-permute-start(bf16[192,512]{1,0:T(8,128)(2,1)S(1)} %get-tuple-element.268), channel_id=1, source_target_pairs={{0,3},{1,2},{2,1},{3,0},{4,7},{5,6},{6,5},{7,4},{8,11},{9,10},{10,... | collective-permute-start | bytes 589832 | tf_op jit(solution)/shard_map/ppermute | solution.py:513
  90.1 9.9 %collective-permute-start.9 = (bf16[192,512]{1,0:T(8,128)(2,1)S(1)}, bf16[192,512]{1,0:T(8,128)(2,1)S(1)}, u32[]{:S(2)}, u32[]{:S(2)}) collective-permute-start(bf16[192,512]{1,0:T(8,128)(2,1)S(1)} %get-tuple-element.267), channel_id=1, source_target_pairs={{0,2},{1,3},{2,0},{3,1},{4,6},{5,7},{6,4},{7,5},{8,10},{9,11},{10,... | collective-permute-start | bytes 589832 | tf_op jit(solution)/shard_map/ppermute | solution.py:513
  90.6 9.6 %collective-permute-start.11 = (bf16[192,768]{1,0:T(8,128)(2,1)}, bf16[192,768]{1,0:T(8,128)(2,1)S(1)}, u32[]{:S(2)}, u32[]{:S(2)}) collective-permute-start(bf16[192,768]{1,0:T(8,128)(2,1)} %collective-permute-done.6), channel_id=1, source_target_pairs={{0,1},{1,0},{2,3},{3,2},{4,5},{5,4},{6,7},{7,6},{8,9},{9,8},{10,11... | collective-permute-start | bytes 884744 | tf_op jit(solution)/shard_map/ppermute | solution.py:513
  91.0 29.6 %collective-permute-start.14 = (bf16[192,2304]{1,0:T(8,128)(2,1)}, bf16[192,2304]{1,0:T(8,128)(2,1)}, u32[]{:S(2)}, u32[]{:S(2)}) collective-permute-start(bf16[192,2304]{1,0:T(8,128)(2,1)} %copy.247), channel_id=1, source_target_pairs={{0,1},{1,0},{2,3},{3,2},{4,5},{5,4},{6,7},{7,6},{8,9},{9,8},{10,11... | collective-permute-start | bytes 2654216 | tf_op jit(solution)/shard_map/ppermute | solution.py:513
  95.3 25.3 %collective-permute-start.13 = (bf16[192,2304]{1,0:T(8,128)(2,1)}, bf16[192,2304]{1,0:T(8,128)(2,1)}, u32[]{:S(2)}, u32[]{:S(2)}) collective-permute-start(bf16[192,2304]{1,0:T(8,128)(2,1)} %collective-permute-done.7), channel_id=1, source_target_pairs={{0,1},{1,0},{2,3},{3,2},{4,5},{5,4},{6,7},{7,6},{8,9},{9,8},{10,11... | collective-permute-start | bytes 2654216 | tf_op jit(solution)/shard_map/ppermute | solution.py:513
  105.1 41.0 %all-to-all-start.1 = ((bf16[8,128,768]{2,1,0:T(8,128)(2,1)}), bf16[8,128,768]{2,1,0:T(8,128)(2,1)S(1)}, u32[]{:S(2)}, u32[]{:S(2)}) async-start(bf16[8,128,768]{2,1,0:T(8,128)(2,1)} %bitcast.200), calls=%async_computation.1 | async-start | bytes 3145728 | tf_op jit(solution)/shard_map/all_to_all | solution.py:509
  181.6 28.9 %collective-permute-start.16 = (bf16[768,1536]{1,0:T(8,128)(2,1)}, bf16[768,1536]{1,0:T(8,128)(2,1)}, u32[]{:S(2)}, u32[]{:S(2)}) collective-permute-start(bf16[768,1536]{1,0:T(8,128)(2,1)} %get-tuple-element.97), channel_id=1, source_target_pairs={{0,1},{1,0},{2,3},{3,2},{4,5},{5,4},{6,7},{7,6},{8,9},{9,8},{10,11... | collective-permute-start | bytes 7077896 | tf_op jit(solution)/shard_map/ppermute | solution.py:513
  193.5 22.8 %collective-permute-start.15 = (bf16[768,1536]{1,0:T(8,128)(2,1)}, bf16[768,1536]{1,0:T(8,128)(2,1)}, u32[]{:S(2)}, u32[]{:S(2)}) collective-permute-start(bf16[768,1536]{1,0:T(8,128)(2,1)} %get-tuple-element.94), channel_id=1, source_target_pairs={{0,1},{1,0},{2,3},{3,2},{4,5},{5,4},{6,7},{7,6},{8,9},{9,8},{10,11... | collective-permute-start | bytes 7077896 | tf_op jit(solution)/shard_map/ppermute | solution.py:513
  194.0 42.0 %all-to-all-start.2 = ((bf16[8,128,768]{2,1,0:T(8,128)(2,1)}), bf16[8,128,768]{2,1,0:T(8,128)(2,1)}, u32[]{:S(2)}, u32[]{:S(2)}) async-start(bf16[8,128,768]{2,1,0:T(8,128)(2,1)} %bitcast.199), calls=%async_computation.2 | async-start | bytes 3145728 | tf_op jit(solution)/shard_map/all_to_all | solution.py:509
  221.7 14.3 %copy-start.12 = (f32[512,768]{1,0:T(8,128)S(1)}, f32[512,768]{1,0:T(8,128)}, u32[]{:S(2)}) copy-start(f32[512,768]{1,0:T(8,128)} %copy-done.10) | copy-start | bytes 4718596
  221.7 14.3 %copy-start.58 = (s32[512]{0:T(512)S(1)}, s32[512]{0:T(512)}, u32[]{:S(2)}) copy-start(s32[512]{0:T(512)} %copy-done.56) | copy-start | bytes 6148
  245.7 8.1 %collective-permute-start.17 = (bf16[192,512]{1,0:T(8,128)(2,1)}, bf16[192,512]{1,0:T(8,128)(2,1)S(1)}, u32[]{:S(2)}, u32[]{:S(2)}) collective-permute-start(bf16[192,512]{1,0:T(8,128)(2,1)} %get-tuple-element.265), channel_id=1, source_target_pairs={{0,3},{1,2},{2,1},{3,0},{4,7},{5,6},{6,5},{7,4},{8,11},{9,10},{10,... | collective-permute-start | bytes 589832 | tf_op jit(solution)/shard_map/ppermute | solution.py:513
  246.1 11.2 %collective-permute-start.18 = (bf16[192,512]{1,0:T(8,128)(2,1)}, bf16[192,512]{1,0:T(8,128)(2,1)S(1)}, u32[]{:S(2)}, u32[]{:S(2)}) collective-permute-start(bf16[192,512]{1,0:T(8,128)(2,1)} %get-tuple-element.264), channel_id=1, source_target_pairs={{0,2},{1,3},{2,0},{3,1},{4,6},{5,7},{6,4},{7,5},{8,10},{9,11},{10,... | collective-permute-start | bytes 589832 | tf_op jit(solution)/shard_map/ppermute | solution.py:513
  247.3 10.6 %collective-permute-start.19 = (bf16[192,512]{1,0:T(8,128)(2,1)}, bf16[192,512]{1,0:T(8,128)(2,1)}, u32[]{:S(2)}, u32[]{:S(2)}) collective-permute-start(bf16[192,512]{1,0:T(8,128)(2,1)} %get-tuple-element.263), channel_id=1, source_target_pairs={{0,1},{1,0},{2,3},{3,2},{4,5},{5,4},{6,7},{7,6},{8,9},{9,8},{10,11... | collective-permute-start | bytes 589832 | tf_op jit(solution)/shard_map/ppermute | solution.py:513
  248.5 42.0 %collective-permute-start.20 = (bf16[8,64,768]{2,1,0:T(8,128)(2,1)}, bf16[8,64,768]{2,1,0:T(8,128)(2,1)}, u32[]{:S(2)}, u32[]{:S(2)}) collective-permute-start(bf16[8,64,768]{2,1,0:T(8,128)(2,1)} %pad_maximum_fusion.7), channel_id=1, source_target_pairs={{0,1},{1,0},{2,3},{3,2},{4,5},{5,4},{6,7},{7,6},{8,9},{9,8},{10,11... | collective-permute-start | bytes 2359304 | tf_op jit(solution)/shard_map/ppermute | solution.py:513
  249.2 49.8 %all-to-all-start.3 = ((bf16[8,128,768]{2,1,0:T(8,128)(2,1)}), bf16[8,128,768]{2,1,0:T(8,128)(2,1)}, u32[]{:S(2)}, u32[]{:S(2)}) async-start(bf16[8,128,768]{2,1,0:T(8,128)(2,1)} %bitcast.197), calls=%async_computation.3 | async-start | bytes 3145728 | tf_op jit(solution)/shard_map/all_to_all | solution.py:509
  259.3 69.3 %collective-permute-start.21 = (bf16[768,768]{1,0:T(8,128)(2,1)}, bf16[768,768]{1,0:T(8,128)(2,1)}, u32[]{:S(2)}, u32[]{:S(2)}) collective-permute-start(bf16[768,768]{1,0:T(8,128)(2,1)} %split.28), channel_id=1, source_target_pairs={{0,2},{1,3},{2,0},{3,1},{4,6},{5,7},{6,4},{7,5},{8,10},{9,11},{10,... | collective-permute-start | bytes 3538952 | tf_op jit(solution)/shard_map/ppermute | solution.py:513
  259.7 68.9 %collective-permute-start.22 = (bf16[768,768]{1,0:T(8,128)(2,1)}, bf16[768,768]{1,0:T(8,128)(2,1)}, u32[]{:S(2)}, u32[]{:S(2)}) collective-permute-start(bf16[768,768]{1,0:T(8,128)(2,1)} %split.27), channel_id=1, source_target_pairs={{0,2},{1,3},{2,0},{3,1},{4,6},{5,7},{6,4},{7,5},{8,10},{9,11},{10,... | collective-permute-start | bytes 3538952 | tf_op jit(solution)/shard_map/ppermute | solution.py:513
  261.4 28.8 %copy-start.55 = (s32[4096]{0:T(1024)S(1)}, s32[4096]{0:T(1024)}, u32[]{:S(2)}) copy-start(s32[4096]{0:T(1024)} %copy-done.54) | copy-start | bytes 49156
  291.7 28.2 %collective-permute-start.23 = (bf16[384,512]{1,0:T(8,128)(2,1)}, bf16[384,512]{1,0:T(8,128)(2,1)}, u32[]{:S(2)}, u32[]{:S(2)}) collective-permute-start(bf16[384,512]{1,0:T(8,128)(2,1)} %get-tuple-element.236), channel_id=1, source_target_pairs={{0,1},{1,0},{2,3},{3,2},{4,5},{5,4},{6,7},{7,6},{8,9},{9,8},{10,11... | collective-permute-start | bytes 1179656 | tf_op jit(solution)/shard_map/ppermute | solution.py:513
  291.7 30.5 %collective-permute-start.24 = (bf16[384,512]{1,0:T(8,128)(2,1)}, bf16[384,512]{1,0:T(8,128)(2,1)}, u32[]{:S(2)}, u32[]{:S(2)}) collective-permute-start(bf16[384,512]{1,0:T(8,128)(2,1)} %get-tuple-element.235), channel_id=1, source_target_pairs={{0,2},{1,3},{2,0},{3,1},{4,6},{5,7},{6,4},{7,5},{8,10},{9,11},{10,... | collective-permute-start | bytes 1179656 | tf_op jit(solution)/shard_map/ppermute | solution.py:513
  292.1 36.5 %collective-permute-start.25 = (bf16[384,512]{1,0:T(8,128)(2,1)}, bf16[384,512]{1,0:T(8,128)(2,1)}, u32[]{:S(2)}, u32[]{:S(2)}) collective-permute-start(bf16[384,512]{1,0:T(8,128)(2,1)} %get-tuple-element.234), channel_id=1, source_target_pairs={{0,3},{1,2},{2,1},{3,0},{4,7},{5,6},{6,5},{7,4},{8,11},{9,10},{10,... | collective-permute-start | bytes 1179656 | tf_op jit(solution)/shard_map/ppermute | solution.py:513
  299.0 40.2 %all-to-all-start.4 = ((bf16[8,112,768]{2,1,0:T(8,128)(2,1)}), bf16[8,112,768]{2,1,0:T(8,128)(2,1)}, u32[]{:S(2)}, u32[]{:S(2)}) async-start(bf16[8,112,768]{2,1,0:T(8,128)(2,1)} %pad_maximum_fusion.2), calls=%async_computation.4 | async-start | bytes 2752512 | tf_op jit(solution)/shard_map/all_to_all | solution.py:509
  305.2 23.4 %slice-start = ((f32[768,1536]{1,0:T(8,128)}), f32[768,768]{1,0:T(8,128)S(1)}, s32[]{:S(2)}) async-start(f32[768,1536]{1,0:T(8,128)} %copy-done.8), calls=%async_computation.6 | async-start | bytes 4718592 | tf_op jit(solution)/shard_map/split | solution.py:675
  340.9 24.8 %all-to-all-start.5 = ((bf16[8,112,192]{1,2,0:T(8,128)(2,1)}), bf16[8,112,192]{1,2,0:T(8,128)(2,1)S(1)}, u32[]{:S(2)}, u32[]{:S(2)}) async-start(bf16[8,112,192]{1,2,0:T(8,128)(2,1)} %pad_maximum_fusion.9), calls=%async_computation.5 | async-start | bytes 786432 | tf_op jit(solution)/shard_map/all_to_all | solution.py:509
  345.3 13.1 %collective-permute-start.32 = (f32[24,777]{1,0:T(8,128)S(1)}, f32[24,777]{1,0:T(8,128)S(1)}, u32[]{:S(2)}, u32[]{:S(2)}) collective-permute-start(f32[24,777]{1,0:T(8,128)S(1)} %pad_maximum_fusion.18), channel_id=1, source_target_pairs={{0,2},{1,3},{2,0},{3,1},{4,6},{5,7},{6,4},{7,5},{8,10},{9,11},{10,... | collective-permute-start | bytes 223784 | tf_op jit(solution)/shard_map/ppermute | solution.py:513
  347.6 12.8 %collective-permute-start.26 = (bf16[192,512]{1,0:T(8,128)(2,1)}, bf16[192,512]{1,0:T(8,128)(2,1)}, u32[]{:S(2)}, u32[]{:S(2)}) collective-permute-start(bf16[192,512]{1,0:T(8,128)(2,1)} %get-tuple-element.262), channel_id=1, source_target_pairs={{0,3},{1,2},{2,1},{3,0},{4,7},{5,6},{6,5},{7,4},{8,11},{9,10},{10,... | collective-permute-start | bytes 589832 | tf_op jit(solution)/shard_map/ppermute | solution.py:513
  348.2 12.2 %collective-permute-start.27 = (bf16[192,512]{1,0:T(8,128)(2,1)}, bf16[192,512]{1,0:T(8,128)(2,1)}, u32[]{:S(2)}, u32[]{:S(2)}) collective-permute-start(bf16[192,512]{1,0:T(8,128)(2,1)} %get-tuple-element.261), channel_id=1, source_target_pairs={{0,2},{1,3},{2,0},{3,1},{4,6},{5,7},{6,4},{7,5},{8,10},{9,11},{10,... | collective-permute-start | bytes 589832 | tf_op jit(solution)/shard_map/ppermute | solution.py:513
  349.9 10.6 %collective-permute-start.28 = (bf16[192,512]{1,0:T(8,128)(2,1)}, bf16[192,512]{1,0:T(8,128)(2,1)}, u32[]{:S(2)}, u32[]{:S(2)}) collective-permute-start(bf16[192,512]{1,0:T(8,128)(2,1)} %get-tuple-element.260), channel_id=1, source_target_pairs={{0,1},{1,0},{2,3},{3,2},{4,5},{5,4},{6,7},{7,6},{8,9},{9,8},{10,11... | collective-permute-start | bytes 589832 | tf_op jit(solution)/shard_map/ppermute | solution.py:513
  366.2 5.2 %collective-permute-start.29 = (f32[32,768]{1,0:T(8,128)S(1)}, f32[32,768]{1,0:T(8,128)S(1)}, u32[]{:S(2)}, u32[]{:S(2)}) collective-permute-start(f32[32,768]{1,0:T(8,128)S(1)} %get-tuple-element.289), channel_id=1, source_target_pairs={{0,3},{1,2},{2,1},{3,0},{4,7},{5,6},{6,5},{7,4},{8,11},{9,10},{10,... | collective-permute-start | bytes 294920 | tf_op jit(solution)/shard_map/ppermute | solution.py:513
  366.8 6.7 %collective-permute-start.30 = (f32[32,768]{1,0:T(8,128)S(1)}, f32[32,768]{1,0:T(8,128)S(1)}, u32[]{:S(2)}, u32[]{:S(2)}) collective-permute-start(f32[32,768]{1,0:T(8,128)S(1)} %get-tuple-element.288), channel_id=1, source_target_pairs={{0,2},{1,3},{2,0},{3,1},{4,6},{5,7},{6,4},{7,5},{8,10},{9,11},{10,... | collective-permute-start | bytes 294920 | tf_op jit(solution)/shard_map/ppermute | solution.py:513
  368.4 5.1 %collective-permute-start.31 = (f32[32,768]{1,0:T(8,128)S(1)}, f32[32,768]{1,0:T(8,128)S(1)}, u32[]{:S(2)}, u32[]{:S(2)}) collective-permute-start(f32[32,768]{1,0:T(8,128)S(1)} %get-tuple-element.287), channel_id=1, source_target_pairs={{0,1},{1,0},{2,3},{3,2},{4,5},{5,4},{6,7},{7,6},{8,9},{9,8},{10,11... | collective-permute-start | bytes 294920 | tf_op jit(solution)/shard_map/ppermute | solution.py:513
  (54 other events, 152.9 us)
where the time goes:
time: 384 us; the launch traced here: 378 us
  Pallas kernels  117 us (30%)
  waiting for transfers between devices  73.5 us (19%)
  starting transfers between devices  52 us (14%)
  local copies, waits for them, and re-layouts  50.8 us (13%)
  matrix products  46.3 us (12%)
  other arithmetic  36.4 us (9%)
    pallas_call x2, Pallas kernels, attention_backward(): pl.pallas_call(backward_kernel, grid=(count,), in_specs=[pl.BlockSpec((1,...  43.2 us
    all_to_all x6, waiting for transfers between devices, exchange(): return lax.all_to_all(rows, axis, split_axis=0, concat_axis=0, tiled=True)  41.1 us
    ppermute x33, waiting for transfers between devices, swap(): lax.ppermute(values, axis, [(i, i ^ step) for i in range(lax.axis_size(ax...  32.3 us
    all_to_all x6, starting transfers between devices, exchange(): return lax.all_to_all(rows, axis, split_axis=0, concat_axis=0, tiled=True)  28.4 us
    pallas_call x1, Pallas kernels, attention_forward(): pl.pallas_call(forward_kernel, grid=(heads,), in_specs=[pl.BlockSpec((1,...  25.4 us
    ppermute x33, starting transfers between devices, swap(): lax.ppermute(values, axis, [(i, i ^ step) for i in range(lax.axis_size(ax...  23.6 us
    pallas_call x1, Pallas kernels, expert_rows(): pl.pallas_call(expert_kernel, grid_spec=pltpu.PrefetchScalarGridSpec(num_...  23.1 us
    unnamed x136, local copies, waits for them, and re-layouts  20.3 us
  transfers between devices with their start and end apart: 39, of which 13 were waited for; matrix products, arithmetic and copies ran while one was open for 27% of the time, Pallas kernels for 21%

commit v1 on v0

--- a/solution.py
+++ b/solution.py
@@ -453,6 +453,41 @@
     )(jnp.stack([owner, here]).astype(jnp.int32), arrived, router, weight, plain)
 
 
+def result_kernel(hidden_ref, weight_ref, result_ref, total_ref):
+    step = pl.program_id(0)
+
+    @pl.when(step == 0)
+    def start():
+        total_ref[...] = jnp.zeros_like(total_ref)
+
+    total_ref[...] += jnp.dot(hidden_ref[...], weight_ref[...], preferred_element_type=f32)
+
+    @pl.when(step == pl.num_programs(0) - 1)
+    def finish():
+        result_ref[...] = total_ref[...].astype(bf16)
+
+
+def expert_results(hidden, weight, steps):
+    slots, depth = hidden.shape
+    width = weight.shape[1]
+    block = depth // steps
+    return pl.pallas_call(
+        result_kernel,
+        grid=(steps,),
+        in_specs=[
+            pl.BlockSpec((slots, block), lambda i: (0, i)),
+            pl.BlockSpec((block, width), lambda i: (i, 0)),
+        ],
+        out_specs=pl.BlockSpec((slots, width), lambda i: (0, 0)),
+        out_shape=jax.ShapeDtypeStruct((slots, width), bf16),
+        scratch_shapes=[pltpu.VMEM((slots, width), f32)],
+        compiler_params=pltpu.CompilerParams(vmem_limit_bytes=48 * 1024 * 1024),
+        cost_estimate=pl.CostEstimate(
+            flops=slots * width, bytes_accessed=1024 * 1024, transcendentals=0
+        ),
+    )(hidden, weight)
+
+
 def weight_grad_kernel(small_ref, big_ref, sent_ref, kept_ref, turned_ref):
     step = pl.program_id(0)
     half = pl.num_programs(0) // 2
@@ -671,7 +706,10 @@
     row_grads_back = send_back(row_grads)
 
     def scatter_first(sent, kept):
-        sums = kept.astype(f32) + swap(sent, 1).astype(f32)
+        return scatter_rest(swap(sent, 1), kept)
+
+    def scatter_rest(got, kept):
+        sums = kept.astype(f32) + got.astype(f32)
         pieces = jnp.split(sums, shards // 2, axis=1)
         step = 2
         while 2 * step < shards:
@@ -685,14 +723,12 @@
     grad_result = (gate * cot_rows.astype(f32)).astype(bf16)
     out_sent, out_kept = weight_grad(grad_result, hidden_sorted, shards)
     in_sent, in_kept = weight_grad(arrived, grad_inner, shards)
-    results = jnp.dot(hidden, weight_out, preferred_element_type=f32).astype(bf16)
+    results = expert_results(hidden, weight_out, shards)
     local_router = lax.dot_general(
         arrived, grad_logits, (((0,), (0,)), ((), ())), preferred_element_type=f32
     )
-    out_kept, out_other = scatter_first(out_sent, out_kept)
-    in_kept, in_other = scatter_first(in_sent, in_kept)
-    row_grads_back, out_other, in_kept, in_other, results, local_router = tie(
-        row_grads_back, out_other, in_kept, in_other, results, local_router
+    row_grads_back, out_sent, out_kept, in_sent, in_kept, results, local_router = tie(
+        row_grads_back, out_sent, out_kept, in_sent, in_kept, results, local_router
     )
     results_back = send_back(results)
 
@@ -731,9 +767,10 @@
     side = here & 1
     rider_kept = rider(side)
     rider_got = swap(rider(1 - side), 1)
-    grad_own, rider_kept, out_other, in_other = tie(grad_own, rider_kept, out_other, in_other)
+    out_kept, out_other = scatter_first(out_sent, out_kept)
+    grad_own, rider_kept, out_other = tie(grad_own, rider_kept, out_other)
     out_got = swap(out_other, shards // 2)
-    in_got = swap(in_other, shards // 2)
+    in_sent = swap(in_sent, 1)
 
     def run_heads(first, count, grad_own):
         grad_qkv, grad_offsets = attention_backward(
@@ -772,7 +809,11 @@
     if early:
         grad_qkv, grad_offsets = run_heads(0, early, grad_own)
         offset_grads.append(grad_offsets)
-        grad_own, grad_qkv, rider_got = tie(grad_own, grad_qkv, rider_got)
+        grad_own, grad_qkv, rider_got, in_sent, out_got = tie(
+            grad_own, grad_qkv, rider_got, in_sent, out_got
+        )
+    in_kept, in_other = scatter_rest(in_sent, in_kept)
+    in_got = swap(in_other, shards // 2)
     riders = (rider_kept.astype(f32) + rider_got.astype(f32)).astype(bf16)
     if early:
         block = attn_in_part(grad_qkv)
@@ -782,8 +823,8 @@
     riders_back = exchange(riders, "expert")
     grad_qkv, grad_offsets = run_heads(early, 1, grad_own)
     if early:
-        grad_qkv, grad_offsets, results_back, out_got, in_got, *pieces = tie(
-            grad_qkv, grad_offsets, results_back, out_got, in_got, *pieces
+        grad_qkv, grad_offsets, results_back, in_got, *pieces = tie(
+            grad_qkv, grad_offsets, results_back, in_got, *pieces
         )
     offset_grads.append(grad_offsets)
     last = attn_in_part(grad_qkv)

time: 384 us -> 375 us (0.977)
  waiting for transfers between devices: 73.5 us -> 59.3 us
  matrix products: 46.3 us -> 37.3 us
  Pallas kernels: 117 us -> 126 us
  other arithmetic: 36.4 us -> 42.9 us
    all_to_all x6, waiting for transfers between devices: 41.1 us -> 29.8 us  [exchange(): return lax.all_to_all(rows, axis, split_axis=0, concat_axis=0, tiled=True)]
    pallas_call x0 -> x1, Pallas kernels: none -> 10.2 us  [expert_results(): pl.pallas_call(result_kernel, grid=(steps,), in_specs=[pl.BlockSpec((slot...]
    dot_general x1 -> x0, matrix products: 9.55 us -> none  [local(): jnp.dot(hidden, weight_out, preferred_element_type=f32).astype(bf16)]
    unnamed x136 -> x138, local copies, waits for them, and re-layouts: 20.3 us -> 19.6 us
  transfers between devices with their start and end apart: 39 -> 39, of which waited for: 13 -> 13; matrix products, arithmetic and copies ran while one was open for 27% -> 28% of each run, Pallas kernels for 21% -> 26%
where the time goes in v1:
time: 375 us; the launch traced here: 369 us
  Pallas kernels  126 us (34%)
  waiting for transfers between devices  59.3 us (16%)
  starting transfers between devices  51.7 us (14%)
  local copies, waits for them, and re-layouts  49.6 us (13%)
  other arithmetic  42.9 us (11%)
  matrix products  37.3 us (10%)
    pallas_call x2, Pallas kernels, attention_backward(): pl.pallas_call(backward_kernel, grid=(count,), in_specs=[pl.BlockSpec((1,...  43.2 us
    all_to_all x6, waiting for transfers between devices, exchange(): return lax.all_to_all(rows, axis, split_axis=0, concat_axis=0, tiled=True)  29.8 us
    ppermute x33, waiting for transfers between devices, swap(): lax.ppermute(values, axis, [(i, i ^ step) for i in range(lax.axis_size(ax...  29.5 us
    all_to_all x6, starting transfers between devices, exchange(): return lax.all_to_all(rows, axis, split_axis=0, concat_axis=0, tiled=True)  28.7 us
    pallas_call x1, Pallas kernels, attention_forward(): pl.pallas_call(forward_kernel, grid=(heads,), in_specs=[pl.BlockSpec((1,...  25.4 us
    pallas_call x1, Pallas kernels, expert_rows(): pl.pallas_call(expert_kernel, grid_spec=pltpu.PrefetchScalarGridSpec(num_...  23.1 us
    ppermute x33, starting transfers between devices, swap(): lax.ppermute(values, axis, [(i, i ^ step) for i in range(lax.axis_size(ax...  23.1 us
    unnamed x138, local copies, waits for them, and re-layouts  19.6 us
  transfers between devices with their start and end apart: 39, of which 13 were waited for; matrix products, arithmetic and copies ran while one was open for 28% of the time, Pallas kernels for 26%

profile of v1, /device:TPU:0, one launch (start us, length us, event | category | flops | bytes accessed | tf_op | source)
XLA Modules:
  0.0 369.4 jit_solution(7039561683736370365)
XLA Ops:
  4.1 3.0 collective-permute-start
  7.1 2.3 copy.240
  9.4 2.4 copy.242
  11.9 2.1 constant_dynamic-slice_fusion.14
  20.0 2.4 copy.241
  22.6 2.2 fusion.8
  28.9 5.9 %collective-permute-done.4.refs_6_ = bf16[192,576]{1,0:T(8,128)(2,1)} collective-permute-done((bf16[192,576]{1,0:T(8,128)(2,1)}, bf16[192,576]{1,0:T(8,128)(2,1)}, u32[]{:S(2)}, u32[]{:S(2)}) %collective-permute-start.4) | collective-permute-done | bytes 221216 | tf_op jit(solution)/shard_map/ppermute | solution.py:548
  34.8 3.6 collective-permute-done.5.refs_7_
  38.4 5.6 %shard_map.195 = (bf16[2048,768]{1,0:T(8,128)(2,1)}, bf16[576,2048]{1,0:T(8,128)(2,1)}) custom-call(s32[1]{0:T(128)} %bitcast.here_ref, f32[1,768]{1,0:T(1,128)S(1)} %reshape.347.gain_ref, bf16[528,768]{1,0:T(8,128)(2,1)S(1)} %constant_dynamic-update-slice_fusion.refs_0_, bf16[528,768]{1,0:T(8,128)(2,1)S(1)} %collective-permute-done.2.refs_1_, ...), custom_call_target="tpu_custom_call" | custom-call | flops 1811939328 | bytes 12582912 | tf_op jit(solution)/shard_map/pallas_call | solution.py:320
  44.0 6.3 %all-to-all-start = ((bf16[8,128,768]{2,1,0:T(8,128)(2,1)}), bf16[8,128,768]{2,1,0:T(8,128)(2,1)}, u32[]{:S(2)}, u32[]{:S(2)}) async-start(bf16[8,128,768]{2,1,0:T(8,128)(2,1)} %bitcast.193), calls=%async_computation | async-start | bytes 3145728 | tf_op jit(solution)/shard_map/all_to_all | solution.py:544
  56.2 25.4 %shard_map.196 = (bf16[192,2048]{1,0:T(8,128)(2,1)S(1)}, f32[3,1,2048]{2,1,0:T(1,128)S(1)}) custom-call(f32[3,32,128]{2,1,0:T(8,128)S(1)} %bitcast.181, bf16[576,2048]{1,0:T(8,128)(2,1)S(1)} %copy-done.6, bf16[576,2048]{1,0:T(8,128)(2,1)S(1)} %copy-done.6, bf16[576,2048]{1,0:T(8,128)(2,1)S(1)} %copy-done.6), custom_call_target="tpu_custom_call" | custom-call | flops 12884901888 | bytes 8388608 | tf_op jit(solution)/shard_map/pallas_call | solution.py:214
  81.7 6.7 %all-to-all-done = bf16[8,128,768]{2,1,0:T(8,128)(2,1)} async-done(((bf16[8,128,768]{2,1,0:T(8,128)(2,1)}), bf16[8,128,768]{2,1,0:T(8,128)(2,1)}, u32[]{:S(2)}, u32[]{:S(2)}) %all-to-all-start) | async-done | bytes 1572896 | tf_op jit(solution)/shard_map/all_to_all | solution.py:544
  91.5 3.9 %collective-permute-done.8 = bf16[192,512]{1,0:T(8,128)(2,1)S(1)} collective-permute-done((bf16[192,512]{1,0:T(8,128)(2,1)S(1)}, bf16[192,512]{1,0:T(8,128)(2,1)S(1)}, u32[]{:S(2)}, u32[]{:S(2)}) %collective-permute-start.8) | collective-permute-done | bytes 196640 | tf_op jit(solution)/shard_map/ppermute | solution.py:548
  96.1 3.8 %collective-permute-done.9 = bf16[192,512]{1,0:T(8,128)(2,1)S(1)} collective-permute-done((bf16[192,512]{1,0:T(8,128)(2,1)S(1)}, bf16[192,512]{1,0:T(8,128)(2,1)S(1)}, u32[]{:S(2)}, u32[]{:S(2)}) %collective-permute-start.9) | collective-permute-done | bytes 196640 | tf_op jit(solution)/shard_map/ppermute | solution.py:548
  102.8 2.3 fusion.9
  105.1 4.2 %all-to-all-start.1 = ((bf16[8,128,768]{2,1,0:T(8,128)(2,1)}), bf16[8,128,768]{2,1,0:T(8,128)(2,1)S(1)}, u32[]{:S(2)}, u32[]{:S(2)}) async-start(bf16[8,128,768]{2,1,0:T(8,128)(2,1)} %bitcast.195), calls=%async_computation.1 | async-start | bytes 3145728 | tf_op jit(solution)/shard_map/all_to_all | solution.py:544
  109.4 10.2 %fusion.45.plain_ref = f32[1024,3072]{1,0:T(8,128)} fusion(bf16[1024,768]{1,0:T(8,128)(2,1)} %bitcast.16, bf16[1,3072,768]{2,1,0:T(8,128)(2,1)} %param.22), kind=kOutput, calls=%fused_computation.219 | convolution fusion | flops 4831838208 | bytes 18874368 | tf_op jit(solution)/shard_map/dot_general | solution.py:697
  120.7 2.3 broadcast_select_fusion.7
  122.9 2.0 pad_maximum_fusion
  124.9 21.2 %all-to-all-done.1 = bf16[8,128,768]{2,1,0:T(8,128)(2,1)S(1)} async-done(((bf16[8,128,768]{2,1,0:T(8,128)(2,1)}), bf16[8,128,768]{2,1,0:T(8,128)(2,1)S(1)}, u32[]{:S(2)}, u32[]{:S(2)}) %all-to-all-start.1) | async-done | bytes 1572896 | tf_op jit(solution)/shard_map/all_to_all | solution.py:544
  147.3 23.1 %shard_map.197 = (bf16[1024,3072]{1,0:T(8,128)(2,1)}, bf16[1024,3072]{1,0:T(8,128)(2,1)}, bf16[1024,3072]{1,0:T(8,128)(2,1)}, bf16[1024,768]{1,0:T(8,128)(2,1)},...) custom-call(s32[2]{0:T(128)S(1)} %pad_add_fusion.1.index_ref, bf16[1024,768]{1,0:T(8,128)(2,1)} %bitcast.177, ...), custom_call_target="tpu_custom_call" | custom-call | flops 9663676416 | bytes 33554432 | tf_op jit(solution)/shard_map/pallas_call | solution.py:413
  170.4 4.5 %all-to-all-start.2 = ((bf16[8,128,768]{2,1,0:T(8,128)(2,1)}), bf16[8,128,768]{2,1,0:T(8,128)(2,1)}, u32[]{:S(2)}, u32[]{:S(2)}) async-start(bf16[8,128,768]{2,1,0:T(8,128)(2,1)} %bitcast.194), calls=%async_computation.2 | async-start | bytes 3145728 | tf_op jit(solution)/shard_map/all_to_all | solution.py:544
  177.4 9.2 %shard_map.199 = (bf16[768,1536]{1,0:T(8,128)(2,1)S(1)}, bf16[768,1536]{1,0:T(8,128)(2,1)}) custom-call(bf16[1024,768]{1,0:T(8,128)(2,1)S(1)} %bitcast.178, bf16[1024,3072]{1,0:T(8,128)(2,1)} %get-tuple-element.96.big_ref), custom_call_target="tpu_custom_call" | custom-call | flops 786432 | bytes 1048576 | tf_op jit(solution)/shard_map/pallas_call | solution.py:514
  189.8 9.4 %shard_map.198 = (bf16[768,1536]{1,0:T(8,128)(2,1)S(1)}, bf16[768,1536]{1,0:T(8,128)(2,1)}) custom-call(bf16[1024,768]{1,0:T(8,128)(2,1)S(1)} %multiply_convert_fusion.small_ref, bf16[1024,3072]{1,0:T(8,128)(2,1)} %get-tuple-element.93.big_ref), custom_call_target="tpu_custom_call" | custom-call | flops 786432 | bytes 1048576 | tf_op jit(solution)/shard_map/pallas_call | solution.py:514
  199.1 10.2 %shard_map.200 = bf16[1024,768]{1,0:T(8,128)(2,1)} custom-call(bf16[1024,3072]{1,0:T(8,128)(2,1)} %get-tuple-element.99.hidden_ref, bf16[3072,768]{1,0:T(8,128)(2,1)} %bitcast.188), custom_call_target="tpu_custom_call" | custom-call | flops 786432 | bytes 1048576 | tf_op jit(solution)/shard_map/pallas_call | solution.py:474
  209.7 1.9 all-to-all-done.2
  211.5 4.4 %multiply_reduce_fusion = (bf16[768]{0:T(1024)(128)(2,1)S(1)}, f32[512]{0:T(512)S(1)}, f32[512,768]{1,0:T(8,128)}) fusion(f32[512,768]{1,0:T(8,128)} %copy-done.10, f32[512]{0:T(512)S(1)} %get-tuple-element.295, f32[768]{0:T(1024)S(1)} %reshape.348, bf16[1024,768]{1,0:T(8,128)(2,1)} %bitcast.26, s32[512]{0:T(512)S(1)} %copy-done.59), kind=kOutput, calls=%fused_computation.33 | convolution fusion | flops 808188672 | bytes 4729344 | tf_op jit(solution)/shard_map/dot_general | solution.py:626
  217.1 1.9 subtract_add_fusion
  225.4 4.5 %all-to-all-start.3 = ((bf16[8,128,768]{2,1,0:T(8,128)(2,1)}), bf16[8,128,768]{2,1,0:T(8,128)(2,1)}, u32[]{:S(2)}, u32[]{:S(2)}) async-start(bf16[8,128,768]{2,1,0:T(8,128)(2,1)} %bitcast.40), calls=%async_computation.3 | async-start | bytes 3145728 | tf_op jit(solution)/shard_map/all_to_all | solution.py:544
  230.1 2.4 collective-permute-done.16
  233.8 4.6 %convert_add_fusion.1 = f32[768,1536]{1,0:T(8,128)} fusion(bf16[768,1536]{1,0:T(8,128)(2,1)} %collective-permute-done.18, bf16[768,1536]{1,0:T(8,128)(2,1)S(1)} %copy-done.24), kind=kLoop, calls=%fused_computation.1 | loop fusion | flops 3538944 | bytes 9437184 | tf_op jit(solution)/shard_map/add | solution.py:712
  238.4 1.9 split.31
  241.9 28.8 %shard_map.201 = (bf16[384,2048]{1,0:T(8,128)(2,1)S(1)}, f32[2,32,128]{2,1,0:T(8,128)S(1)}) custom-call(f32[3,32,128]{2,1,0:T(8,128)S(1)} %bitcast.182, bf16[576,2048]{1,0:T(8,128)(2,1)S(1)} %copy-done.7, bf16[576,2048]{1,0:T(8,128)(2,1)S(1)} %copy-done.7, bf16[576,2048]{1,0:T(8,128)(2,1)S(1)} %copy-done.7, ...), custom_call_target="tpu_custom_call" | custom-call | flops 37580963840 | bytes 4194304 | tf_op jit(solution)/shard_map/pallas_call | solution.py:254
  273.5 2.3 convert_add_fusion
  275.8 2.2 copy-done.9
  288.2 4.5 %all-to-all-start.4 = ((bf16[8,112,768]{2,1,0:T(8,128)(2,1)}), bf16[8,112,768]{2,1,0:T(8,128)(2,1)}, u32[]{:S(2)}, u32[]{:S(2)}) async-start(bf16[8,112,768]{2,1,0:T(8,128)(2,1)} %pad_maximum_fusion.2), calls=%async_computation.4 | async-start | bytes 2752512 | tf_op jit(solution)/shard_map/all_to_all | solution.py:544
  294.4 14.4 %shard_map.202 = (bf16[192,2048]{1,0:T(8,128)(2,1)S(1)}, f32[1,32,128]{2,1,0:T(8,128)S(1)}) custom-call(f32[3,32,128]{2,1,0:T(8,128)S(1)} %bitcast.183, bf16[576,2048]{1,0:T(8,128)(2,1)S(1)} %copy-done.8, bf16[576,2048]{1,0:T(8,128)(2,1)S(1)} %copy-done.8, bf16[576,2048]{1,0:T(8,128)(2,1)S(1)} %copy-done.8, ...), custom_call_target="tpu_custom_call" | custom-call | flops 18790481920 | bytes 4194304 | tf_op jit(solution)/shard_map/pallas_call | solution.py:254
  308.8 3.3 fusion
  312.1 3.0 copy.277
  316.8 5.5 %collective-permute-done.25 = bf16[384,512]{1,0:T(8,128)(2,1)} collective-permute-done((bf16[384,512]{1,0:T(8,128)(2,1)}, bf16[384,512]{1,0:T(8,128)(2,1)}, u32[]{:S(2)}, u32[]{:S(2)}) %collective-permute-start.25) | collective-permute-done | bytes 393248 | tf_op jit(solution)/shard_map/ppermute | solution.py:548
  322.3 2.7 convolution_convert_fusion.3
  326.9 3.6 fusion.1
  332.1 4.6 %all-to-all-start.5 = ((bf16[8,112,192]{1,2,0:T(8,128)(2,1)}), bf16[8,112,192]{1,2,0:T(8,128)(2,1)S(1)}, u32[]{:S(2)}, u32[]{:S(2)}) async-start(bf16[8,112,192]{1,2,0:T(8,128)(2,1)} %pad_maximum_fusion.9), calls=%async_computation.5 | async-start | bytes 786432 | tf_op jit(solution)/shard_map/all_to_all | solution.py:544
  343.5 2.6 fusion.2
  346.1 3.6 add_convert_fusion
  353.6 3.3 fusion.10
  359.7 2.9 fusion.13
  362.7 2.1 collective-permute-done.30
  (334 shorter events, 81.4 us)
Async XLA Ops:
  0.6 50.0 %copy-start = (bf16[32,12]{0,1:T(8,128)(2,1)S(1)}, bf16[32,12]{0,1:T(8,128)(2,1)}, u32[]{:S(2)}) copy-start(bf16[32,12]{0,1:T(8,128)(2,1)} %param.16) | copy-start | bytes 2308
  4.1 21.1 %collective-permute-start = (bf16[528,768]{1,0:T(8,128)(2,1)S(1)}, bf16[528,768]{1,0:T(8,128)(2,1)S(1)}, u32[]{:S(2)}, u32[]{:S(2)}) collective-permute-start(bf16[528,768]{1,0:T(8,128)(2,1)S(1)} %constant_dynamic-update-slice_fusion.refs_0_), channel_id=1, source_target_pairs={{0,2},{1,3},{2,0},{3,1},{4,6},{5,7},{6,4},{7,5},{8,10},{9,11},{10,... | collective-permute-start | bytes 2433032 | tf_op jit(solution)/shard_map/ppermute | solution.py:548
  7.1 20.3 %collective-permute-start.2 = (bf16[528,768]{1,0:T(8,128)(2,1)S(1)}, bf16[528,768]{1,0:T(8,128)(2,1)S(1)}, u32[]{:S(2)}, u32[]{:S(2)}) collective-permute-start(bf16[528,768]{1,0:T(8,128)(2,1)S(1)} %constant_dynamic-update-slice_fusion.refs_0_), channel_id=1, source_target_pairs={{0,1},{1,0},{2,3},{3,2},{4,5},{5,4},{6,7},{7,6},{8,9},{9,8},{10,11... | collective-permute-start | bytes 2433032 | tf_op jit(solution)/shard_map/ppermute | solution.py:548
  25.2 2.7 collective-permute-start.1
  25.3 3.6 collective-permute-start.3
  25.7 9.1 %collective-permute-start.4 = (bf16[192,576]{1,0:T(8,128)(2,1)}, bf16[192,576]{1,0:T(8,128)(2,1)}, u32[]{:S(2)}, u32[]{:S(2)}) collective-permute-start(bf16[192,576]{1,0:T(8,128)(2,1)} %bitcast.14), channel_id=1, source_target_pairs={{0,2},{1,3},{2,0},{3,1},{4,6},{5,7},{6,4},{7,5},{8,10},{9,11},{10,... | collective-permute-start | bytes 663560 | tf_op jit(solution)/shard_map/ppermute | solution.py:548
  27.4 11.0 %collective-permute-start.5 = (bf16[192,576]{1,0:T(8,128)(2,1)}, bf16[192,576]{1,0:T(8,128)(2,1)}, u32[]{:S(2)}, u32[]{:S(2)}) collective-permute-start(bf16[192,576]{1,0:T(8,128)(2,1)} %bitcast.15), channel_id=1, source_target_pairs={{0,3},{1,2},{2,1},{3,0},{4,7},{5,6},{6,5},{7,4},{8,11},{9,10},{10,... | collective-permute-start | bytes 663560 | tf_op jit(solution)/shard_map/ppermute | solution.py:548
  44.0 44.3 %all-to-all-start = ((bf16[8,128,768]{2,1,0:T(8,128)(2,1)}), bf16[8,128,768]{2,1,0:T(8,128)(2,1)}, u32[]{:S(2)}, u32[]{:S(2)}) async-start(bf16[8,128,768]{2,1,0:T(8,128)(2,1)} %bitcast.193), calls=%async_computation | async-start | bytes 3145728 | tf_op jit(solution)/shard_map/all_to_all | solution.py:544
  50.9 30.7 %collective-permute-start.6 = (bf16[192,768]{1,0:T(8,128)(2,1)S(1)}, bf16[192,768]{1,0:T(8,128)(2,1)}, u32[]{:S(2)}, u32[]{:S(2)}) collective-permute-start(bf16[192,768]{1,0:T(8,128)(2,1)S(1)} %copy-done.38), channel_id=1, source_target_pairs={{0,2},{1,3},{2,0},{3,1},{4,6},{5,7},{6,4},{7,5},{8,10},{9,11},{10,... | collective-permute-start | bytes 884744 | tf_op jit(solution)/shard_map/ppermute | solution.py:548
  52.5 47.8 %collective-permute-start.12 = (bf16[192,768]{1,0:T(8,128)(2,1)S(1)}, bf16[192,768]{1,0:T(8,128)(2,1)}, u32[]{:S(2)}, u32[]{:S(2)}) collective-permute-start(bf16[192,768]{1,0:T(8,128)(2,1)S(1)} %copy-done.38), channel_id=1, source_target_pairs={{0,1},{1,0},{2,3},{3,2},{4,5},{5,4},{6,7},{7,6},{8,9},{9,8},{10,11... | collective-permute-start | bytes 884744 | tf_op jit(solution)/shard_map/ppermute | solution.py:548
  54.0 27.6 %collective-permute-start.7 = (bf16[192,2304]{1,0:T(8,128)(2,1)}, bf16[192,2304]{1,0:T(8,128)(2,1)}, u32[]{:S(2)}, u32[]{:S(2)}) collective-permute-start(bf16[192,2304]{1,0:T(8,128)(2,1)} %copy.247), channel_id=1, source_target_pairs={{0,2},{1,3},{2,0},{3,1},{4,6},{5,7},{6,4},{7,5},{8,10},{9,11},{10,... | collective-permute-start | bytes 2654216 | tf_op jit(solution)/shard_map/ppermute | solution.py:548
  56.2 34.4 %copy-start.33 = (bf16[1,1,16,768]{3,1,2,0:T(2,128)(2,1)S(1)}, bf16[1,1,16,768]{3,1,2,0:T(2,128)(2,1)}, u32[]{:S(2)}) copy-start(bf16[1,1,16,768]{3,1,2,0:T(2,128)(2,1)} %copy-done.32) | copy-start | bytes 73732
  56.2 34.4 %copy-start.35 = (bf16[1,1,16,768]{3,1,2,0:T(2,128)(2,1)S(1)}, bf16[1,1,16,768]{3,1,2,0:T(2,128)(2,1)}, u32[]{:S(2)}) copy-start(bf16[1,1,16,768]{3,1,2,0:T(2,128)(2,1)} %copy-done.34) | copy-start | bytes 73732
  56.2 34.4 %copy-start.37 = (bf16[1,1,16,768]{3,1,2,0:T(2,128)(2,1)S(1)}, bf16[1,1,16,768]{3,1,2,0:T(2,128)(2,1)}, u32[]{:S(2)}) copy-start(bf16[1,1,16,768]{3,1,2,0:T(2,128)(2,1)} %copy-done.36) | copy-start | bytes 73732
  56.2 34.7 %copy-start.56 = (f32[4,192]{1,0:T(4,128)S(1)}, f32[4,192]{1,0:T(4,128)}, u32[]{:S(2)}) copy-start(f32[4,192]{1,0:T(4,128)} %get-tuple-element.281) | copy-start | bytes 9220
  88.4 2.6 collective-permute-start.10
  88.5 6.8 %collective-permute-start.8 = (bf16[192,512]{1,0:T(8,128)(2,1)S(1)}, bf16[192,512]{1,0:T(8,128)(2,1)S(1)}, u32[]{:S(2)}, u32[]{:S(2)}) collective-permute-start(bf16[192,512]{1,0:T(8,128)(2,1)S(1)} %get-tuple-element.270), channel_id=1, source_target_pairs={{0,3},{1,2},{2,1},{3,0},{4,7},{5,6},{6,5},{7,4},{8,11},{9,10},{10,... | collective-permute-start | bytes 589832 | tf_op jit(solution)/shard_map/ppermute | solution.py:548
  90.1 9.9 %collective-permute-start.9 = (bf16[192,512]{1,0:T(8,128)(2,1)S(1)}, bf16[192,512]{1,0:T(8,128)(2,1)S(1)}, u32[]{:S(2)}, u32[]{:S(2)}) collective-permute-start(bf16[192,512]{1,0:T(8,128)(2,1)S(1)} %get-tuple-element.269), channel_id=1, source_target_pairs={{0,2},{1,3},{2,0},{3,1},{4,6},{5,7},{6,4},{7,5},{8,10},{9,11},{10,... | collective-permute-start | bytes 589832 | tf_op jit(solution)/shard_map/ppermute | solution.py:548
  90.6 9.6 %collective-permute-start.11 = (bf16[192,768]{1,0:T(8,128)(2,1)}, bf16[192,768]{1,0:T(8,128)(2,1)S(1)}, u32[]{:S(2)}, u32[]{:S(2)}) collective-permute-start(bf16[192,768]{1,0:T(8,128)(2,1)} %collective-permute-done.6), channel_id=1, source_target_pairs={{0,1},{1,0},{2,3},{3,2},{4,5},{5,4},{6,7},{7,6},{8,9},{9,8},{10,11... | collective-permute-start | bytes 884744 | tf_op jit(solution)/shard_map/ppermute | solution.py:548
  91.0 29.7 %collective-permute-start.14 = (bf16[192,2304]{1,0:T(8,128)(2,1)}, bf16[192,2304]{1,0:T(8,128)(2,1)}, u32[]{:S(2)}, u32[]{:S(2)}) collective-permute-start(bf16[192,2304]{1,0:T(8,128)(2,1)} %copy.247), channel_id=1, source_target_pairs={{0,1},{1,0},{2,3},{3,2},{4,5},{5,4},{6,7},{7,6},{8,9},{9,8},{10,11... | collective-permute-start | bytes 2654216 | tf_op jit(solution)/shard_map/ppermute | solution.py:548
  95.3 25.3 %collective-permute-start.13 = (bf16[192,2304]{1,0:T(8,128)(2,1)}, bf16[192,2304]{1,0:T(8,128)(2,1)}, u32[]{:S(2)}, u32[]{:S(2)}) collective-permute-start(bf16[192,2304]{1,0:T(8,128)(2,1)} %collective-permute-done.7), channel_id=1, source_target_pairs={{0,1},{1,0},{2,3},{3,2},{4,5},{5,4},{6,7},{7,6},{8,9},{9,8},{10,11... | collective-permute-start | bytes 2654216 | tf_op jit(solution)/shard_map/ppermute | solution.py:548
  105.1 41.0 %all-to-all-start.1 = ((bf16[8,128,768]{2,1,0:T(8,128)(2,1)}), bf16[8,128,768]{2,1,0:T(8,128)(2,1)S(1)}, u32[]{:S(2)}, u32[]{:S(2)}) async-start(bf16[8,128,768]{2,1,0:T(8,128)(2,1)} %bitcast.195), calls=%async_computation.1 | async-start | bytes 3145728 | tf_op jit(solution)/shard_map/all_to_all | solution.py:544
  109.3 10.3 %copy-start.11 = (f32[512,768]{1,0:T(8,128)S(1)}, f32[512,768]{1,0:T(8,128)}, u32[]{:S(2)}) copy-start(f32[512,768]{1,0:T(8,128)} %copy-done.10) | copy-start | bytes 4718596
  170.4 41.1 %all-to-all-start.2 = ((bf16[8,128,768]{2,1,0:T(8,128)(2,1)}), bf16[8,128,768]{2,1,0:T(8,128)(2,1)}, u32[]{:S(2)}, u32[]{:S(2)}) async-start(bf16[8,128,768]{2,1,0:T(8,128)(2,1)} %bitcast.194), calls=%async_computation.2 | async-start | bytes 3145728 | tf_op jit(solution)/shard_map/all_to_all | solution.py:544
  199.1 10.2 %copy-start.5 = (bf16[768,1536]{1,0:T(8,128)(2,1)}, bf16[768,1536]{1,0:T(8,128)(2,1)S(1)}, u32[]{:S(2)}) copy-start(bf16[768,1536]{1,0:T(8,128)(2,1)S(1)} %get-tuple-element.104) | copy-start | bytes 7077892
  216.2 17.6 %collective-permute-start.18 = (bf16[768,1536]{1,0:T(8,128)(2,1)}, bf16[768,1536]{1,0:T(8,128)(2,1)}, u32[]{:S(2)}, u32[]{:S(2)}) collective-permute-start(bf16[768,1536]{1,0:T(8,128)(2,1)} %copy-done.5), channel_id=1, source_target_pairs={{0,1},{1,0},{2,3},{3,2},{4,5},{5,4},{6,7},{7,6},{8,9},{9,8},{10,11... | collective-permute-start | bytes 7077896 | tf_op jit(solution)/shard_map/ppermute | solution.py:548
  220.8 9.2 %collective-permute-start.15 = (bf16[192,512]{1,0:T(8,128)(2,1)}, bf16[192,512]{1,0:T(8,128)(2,1)S(1)}, u32[]{:S(2)}, u32[]{:S(2)}) collective-permute-start(bf16[192,512]{1,0:T(8,128)(2,1)} %get-tuple-element.267), channel_id=1, source_target_pairs={{0,3},{1,2},{2,1},{3,0},{4,7},{5,6},{6,5},{7,4},{8,11},{9,10},{10,... | collective-permute-start | bytes 589832 | tf_op jit(solution)/shard_map/ppermute | solution.py:548
  222.1 10.5 %collective-permute-start.16 = (bf16[192,512]{1,0:T(8,128)(2,1)}, bf16[192,512]{1,0:T(8,128)(2,1)}, u32[]{:S(2)}, u32[]{:S(2)}) collective-permute-start(bf16[192,512]{1,0:T(8,128)(2,1)} %get-tuple-element.266), channel_id=1, source_target_pairs={{0,2},{1,3},{2,0},{3,1},{4,6},{5,7},{6,4},{7,5},{8,10},{9,11},{10,... | collective-permute-start | bytes 589832 | tf_op jit(solution)/shard_map/ppermute | solution.py:548
  222.6 9.9 %collective-permute-start.17 = (bf16[192,512]{1,0:T(8,128)(2,1)}, bf16[192,512]{1,0:T(8,128)(2,1)}, u32[]{:S(2)}, u32[]{:S(2)}) collective-permute-start(bf16[192,512]{1,0:T(8,128)(2,1)} %get-tuple-element.265), channel_id=1, source_target_pairs={{0,1},{1,0},{2,3},{3,2},{4,5},{5,4},{6,7},{7,6},{8,9},{9,8},{10,11... | collective-permute-start | bytes 589832 | tf_op jit(solution)/shard_map/ppermute | solution.py:548
  224.5 46.5 %collective-permute-start.19 = (bf16[8,64,768]{2,1,0:T(8,128)(2,1)}, bf16[8,64,768]{2,1,0:T(8,128)(2,1)}, u32[]{:S(2)}, u32[]{:S(2)}) collective-permute-start(bf16[8,64,768]{2,1,0:T(8,128)(2,1)} %pad_maximum_fusion.7), channel_id=1, source_target_pairs={{0,1},{1,0},{2,3},{3,2},{4,5},{5,4},{6,7},{7,6},{8,9},{9,8},{10,11... | collective-permute-start | bytes 2359304 | tf_op jit(solution)/shard_map/ppermute | solution.py:548
  225.4 62.8 %all-to-all-start.3 = ((bf16[8,128,768]{2,1,0:T(8,128)(2,1)}), bf16[8,128,768]{2,1,0:T(8,128)(2,1)}, u32[]{:S(2)}, u32[]{:S(2)}) async-start(bf16[8,128,768]{2,1,0:T(8,128)(2,1)} %bitcast.40), calls=%async_computation.3 | async-start | bytes 3145728 | tf_op jit(solution)/shard_map/all_to_all | solution.py:544
  230.0 41.0 %collective-permute-start.20 = (bf16[768,1536]{1,0:T(8,128)(2,1)}, bf16[768,1536]{1,0:T(8,128)(2,1)S(1)}, u32[]{:S(2)}, u32[]{:S(2)}) collective-permute-start(bf16[768,1536]{1,0:T(8,128)(2,1)} %copy-done.4), channel_id=1, source_target_pairs={{0,1},{1,0},{2,3},{3,2},{4,5},{5,4},{6,7},{7,6},{8,9},{9,8},{10,11... | collective-permute-start | bytes 7077896 | tf_op jit(solution)/shard_map/ppermute | solution.py:548
  240.3 30.7 %collective-permute-start.21 = (bf16[768,768]{1,0:T(8,128)(2,1)S(1)}, bf16[768,768]{1,0:T(8,128)(2,1)S(1)}, u32[]{:S(2)}, u32[]{:S(2)}) collective-permute-start(bf16[768,768]{1,0:T(8,128)(2,1)S(1)} %split.31), channel_id=1, source_target_pairs={{0,2},{1,3},{2,0},{3,1},{4,6},{5,7},{6,4},{7,5},{8,10},{9,11},{10,... | collective-permute-start | bytes 3538952 | tf_op jit(solution)/shard_map/ppermute | solution.py:548
  241.9 31.6 %copy-start.23 = (bf16[768,1536]{1,0:T(8,128)(2,1)S(1)}, bf16[768,1536]{1,0:T(8,128)(2,1)}, u32[]{:S(2)}) copy-start(bf16[768,1536]{1,0:T(8,128)(2,1)} %get-tuple-element.114) | copy-start | bytes 7077892
  279.2 43.2 %collective-permute-start.22 = (bf16[768,768]{1,0:T(8,128)(2,1)}, bf16[768,768]{1,0:T(8,128)(2,1)}, u32[]{:S(2)}, u32[]{:S(2)}) collective-permute-start(bf16[768,768]{1,0:T(8,128)(2,1)} %split.30), channel_id=1, source_target_pairs={{0,2},{1,3},{2,0},{3,1},{4,6},{5,7},{6,4},{7,5},{8,10},{9,11},{10,... | collective-permute-start | bytes 3538952 | tf_op jit(solution)/shard_map/ppermute | solution.py:548
  280.9 34.6 %collective-permute-start.23 = (bf16[384,512]{1,0:T(8,128)(2,1)}, bf16[384,512]{1,0:T(8,128)(2,1)}, u32[]{:S(2)}, u32[]{:S(2)}) collective-permute-start(bf16[384,512]{1,0:T(8,128)(2,1)} %get-tuple-element.238), channel_id=1, source_target_pairs={{0,1},{1,0},{2,3},{3,2},{4,5},{5,4},{6,7},{7,6},{8,9},{9,8},{10,11... | collective-permute-start | bytes 1179656 | tf_op jit(solution)/shard_map/ppermute | solution.py:548
  280.9 35.9 %collective-permute-start.24 = (bf16[384,512]{1,0:T(8,128)(2,1)}, bf16[384,512]{1,0:T(8,128)(2,1)}, u32[]{:S(2)}, u32[]{:S(2)}) collective-permute-start(bf16[384,512]{1,0:T(8,128)(2,1)} %get-tuple-element.237), channel_id=1, source_target_pairs={{0,2},{1,3},{2,0},{3,1},{4,6},{5,7},{6,4},{7,5},{8,10},{9,11},{10,... | collective-permute-start | bytes 1179656 | tf_op jit(solution)/shard_map/ppermute | solution.py:548
  282.4 39.9 %collective-permute-start.25 = (bf16[384,512]{1,0:T(8,128)(2,1)}, bf16[384,512]{1,0:T(8,128)(2,1)}, u32[]{:S(2)}, u32[]{:S(2)}) collective-permute-start(bf16[384,512]{1,0:T(8,128)(2,1)} %get-tuple-element.236), channel_id=1, source_target_pairs={{0,3},{1,2},{2,1},{3,0},{4,7},{5,6},{6,5},{7,4},{8,11},{9,10},{10,... | collective-permute-start | bytes 1179656 | tf_op jit(solution)/shard_map/ppermute | solution.py:548
  288.2 42.3 %all-to-all-start.4 = ((bf16[8,112,768]{2,1,0:T(8,128)(2,1)}), bf16[8,112,768]{2,1,0:T(8,128)(2,1)}, u32[]{:S(2)}, u32[]{:S(2)}) async-start(bf16[8,112,768]{2,1,0:T(8,128)(2,1)} %pad_maximum_fusion.2), calls=%async_computation.4 | async-start | bytes 2752512 | tf_op jit(solution)/shard_map/all_to_all | solution.py:544
  294.4 14.4 %copy-start.28 = (bf16[768,768]{1,0:T(8,128)(2,1)S(1)}, bf16[768,768]{1,0:T(8,128)(2,1)}, u32[]{:S(2)}) copy-start(bf16[768,768]{1,0:T(8,128)(2,1)} %copy-done.27) | copy-start | bytes 3538948
  332.1 24.9 %all-to-all-start.5 = ((bf16[8,112,192]{1,2,0:T(8,128)(2,1)}), bf16[8,112,192]{1,2,0:T(8,128)(2,1)S(1)}, u32[]{:S(2)}, u32[]{:S(2)}) async-start(bf16[8,112,192]{1,2,0:T(8,128)(2,1)} %pad_maximum_fusion.9), calls=%async_computation.5 | async-start | bytes 786432 | tf_op jit(solution)/shard_map/all_to_all | solution.py:544
  336.9 12.8 %collective-permute-start.32 = (f32[24,777]{1,0:T(8,128)S(1)}, f32[24,777]{1,0:T(8,128)S(1)}, u32[]{:S(2)}, u32[]{:S(2)}) collective-permute-start(f32[24,777]{1,0:T(8,128)S(1)} %pad_maximum_fusion.18), channel_id=1, source_target_pairs={{0,2},{1,3},{2,0},{3,1},{4,6},{5,7},{6,4},{7,5},{8,10},{9,11},{10,... | collective-permute-start | bytes 223784 | tf_op jit(solution)/shard_map/ppermute | solution.py:548
  338.8 12.9 %collective-permute-start.26 = (bf16[192,512]{1,0:T(8,128)(2,1)}, bf16[192,512]{1,0:T(8,128)(2,1)}, u32[]{:S(2)}, u32[]{:S(2)}) collective-permute-start(bf16[192,512]{1,0:T(8,128)(2,1)} %get-tuple-element.264), channel_id=1, source_target_pairs={{0,3},{1,2},{2,1},{3,0},{4,7},{5,6},{6,5},{7,4},{8,11},{9,10},{10,... | collective-permute-start | bytes 589832 | tf_op jit(solution)/shard_map/ppermute | solution.py:548
  340.5 11.2 %collective-permute-start.27 = (bf16[192,512]{1,0:T(8,128)(2,1)}, bf16[192,512]{1,0:T(8,128)(2,1)}, u32[]{:S(2)}, u32[]{:S(2)}) collective-permute-start(bf16[192,512]{1,0:T(8,128)(2,1)} %get-tuple-element.263), channel_id=1, source_target_pairs={{0,2},{1,3},{2,0},{3,1},{4,6},{5,7},{6,4},{7,5},{8,10},{9,11},{10,... | collective-permute-start | bytes 589832 | tf_op jit(solution)/shard_map/ppermute | solution.py:548
  341.1 10.6 %collective-permute-start.28 = (bf16[192,512]{1,0:T(8,128)(2,1)}, bf16[192,512]{1,0:T(8,128)(2,1)}, u32[]{:S(2)}, u32[]{:S(2)}) collective-permute-start(bf16[192,512]{1,0:T(8,128)(2,1)} %get-tuple-element.262), channel_id=1, source_target_pairs={{0,1},{1,0},{2,3},{3,2},{4,5},{5,4},{6,7},{7,6},{8,9},{9,8},{10,11... | collective-permute-start | bytes 589832 | tf_op jit(solution)/shard_map/ppermute | solution.py:548
  357.5 5.1 %collective-permute-start.29 = (f32[32,768]{1,0:T(8,128)S(1)}, f32[32,768]{1,0:T(8,128)S(1)}, u32[]{:S(2)}, u32[]{:S(2)}) collective-permute-start(f32[32,768]{1,0:T(8,128)S(1)} %get-tuple-element.291), channel_id=1, source_target_pairs={{0,3},{1,2},{2,1},{3,0},{4,7},{5,6},{6,5},{7,4},{8,11},{9,10},{10,... | collective-permute-start | bytes 294920 | tf_op jit(solution)/shard_map/ppermute | solution.py:548
  359.1 5.7 %collective-permute-start.30 = (f32[32,768]{1,0:T(8,128)S(1)}, f32[32,768]{1,0:T(8,128)S(1)}, u32[]{:S(2)}, u32[]{:S(2)}) collective-permute-start(f32[32,768]{1,0:T(8,128)S(1)} %get-tuple-element.290), channel_id=1, source_target_pairs={{0,2},{1,3},{2,0},{3,1},{4,6},{5,7},{6,4},{7,5},{8,10},{9,11},{10,... | collective-permute-start | bytes 294920 | tf_op jit(solution)/shard_map/ppermute | solution.py:548
  359.7 5.1 %collective-permute-start.31 = (f32[32,768]{1,0:T(8,128)S(1)}, f32[32,768]{1,0:T(8,128)S(1)}, u32[]{:S(2)}, u32[]{:S(2)}) collective-permute-start(f32[32,768]{1,0:T(8,128)S(1)} %get-tuple-element.289), channel_id=1, source_target_pairs={{0,1},{1,0},{2,3},{3,2},{4,5},{5,4},{6,7},{7,6},{8,9},{9,8},{10,11... | collective-permute-start | bytes 294920 | tf_op jit(solution)/shard_map/ppermute | solution.py:548
  (54 other events, 142.9 us)
